TPU v7x, 32 devices: a whole 2x2x4 slice. The times are simulated.
32 devices in a mesh: brick: 8 (over z, y), mp: 4 (over x, core).
Axes of the slice: x: 2, y: 2, z: 4, core: 2. Of those that a mesh axis runs over, the one named last changes fastest.
Arguments:
- voxel_feats: bfloat16 [24576, 512], P('brick'), may hold values from -6 to 6
- slot_rank: int32 [24576], P('brick'), may hold values from 0 to 16384, as said below
- curve_order: int32 [16384], P('brick'), may hold values from 0 to 24575, as said below
- patch_shift: int32 [1], replicated, may hold values from 1 to 1023
- qkv_weight: bfloat16 [512, 1536], P(None, 'mp')
- proj_weight: bfloat16 [512, 512], P('mp'), may hold values from -0.25 to 0.25
- up_weight: bfloat16 [512, 2048], P(None, 'mp'), may hold values from -0.25 to 0.25
- down_weight: bfloat16 [2048, 512], P('mp'), may hold values from -0.125 to 0.125
- norm_gains: float32 [2, 512], replicated, may hold values from 0.25 to 1.75
Outputs:
- voxel_out: bfloat16 [24576, 512], P('brick', 'mp')
Inputs may be any that keep to these rules, and one draw needn't show every extreme that they name: `slot_rank`: within each brick's 3072 slots the occupied ones come first and hold distinct curve positions in increasing order; the rest hold 16384. Every curve position lies in exactly one slot. Curve shard k is positions k * 2048 to (k + 1) * 2048 - 1 and draws its voxels only from bricks k - 1, k, k + 1 and k + 2 (mod 8). A brick holds at most 768 voxels of one shard, and some brick holds exactly 768 of some shard; some brick has all 3072 slots occupied. curve_order[p] = brick * 3072 + slot of the voxel at curve position p, the inverse of slot_rank on occupied slots.
All inputs are finite; a program needn't handle non-finite values.
Results may differ from a plain program's by a relative error of at most 0.012.
The roundings to bfloat16 on the way count: a program that leaves them out, or rounds other values in their place, can miss the bound.
Values may be sent and summed in bfloat16 or wider, within the bound.
A program may use at most 128 MiB of HBM per device.

v0:
```python
import math

import jax
import jax.numpy as jnp
from jax import lax
from jax.sharding import PartitionSpec as P

HEADS = 32
PATCH = 1024


EPSILON = 1e-05


def shifted(value, axis, steps):
    count = lax.axis_size(axis)
    pairs = [(source, (source + steps) % count) for source in range(count)]
    return lax.ppermute(value, axis, pairs)


def layer_norm(values, gain):
    values = values.astype(jnp.float32)
    centred = values - jnp.mean(values, axis=-1, keepdims=True)
    spread = jnp.mean(centred * centred, axis=-1, keepdims=True)
    return (centred * lax.rsqrt(spread + EPSILON) * gain).astype(jnp.bfloat16)


def patch_attention(qkv_rows, heads_here, patch_len):
    row_count = qkv_rows.shape[0]
    head_dim = qkv_rows.shape[1] // (3 * heads_here)
    group_size = math.gcd(heads_here, 4)
    group_count = heads_here // group_size
    scale = head_dim ** (-0.5)

    def one_group(piece):
        scores = (
            jnp.einsum(
                "qhd,khd->hqk", piece[:, :, 0], piece[:, :, 1], preferred_element_type=jnp.float32
            )
            * scale
        )
        highest = jnp.max(scores, axis=-1, keepdims=True)
        weights_exp = jnp.exp(scores - highest)
        softmax_weights = (weights_exp / jnp.sum(weights_exp, axis=-1, keepdims=True)).astype(
            jnp.bfloat16
        )
        return jnp.einsum(
            "hqk,khd->qhd", softmax_weights, piece[:, :, 2], preferred_element_type=jnp.float32
        ).astype(jnp.bfloat16)

    def one_patch(block):
        pieces = jnp.moveaxis(block.reshape(patch_len, group_count, group_size, 3, head_dim), 1, 0)
        outputs = lax.map(one_group, pieces)
        return jnp.moveaxis(outputs, 0, 1).reshape(patch_len, heads_here * head_dim)

    blocks = qkv_rows.reshape(row_count // patch_len, patch_len, qkv_rows.shape[1])
    return lax.map(one_patch, blocks).reshape(row_count, heads_here * head_dim)


def per_device(
    voxel_feats,
    slot_rank,
    curve_order,
    patch_shift,
    qkv_weight,
    proj_weight,
    up_weight,
    down_weight,
    norm_gains,
):
    bricks = lax.axis_size("brick")
    model_parts = lax.axis_size("mp")
    my_index = lax.axis_index("brick")
    capacity = voxel_feats.shape[0]
    shard_rows = curve_order.shape[0]
    all_rows = shard_rows * bricks
    pair_rows = 3 * (shard_rows // 8)
    width_full = voxel_feats.shape[1]
    width_part = width_full // model_parts
    offset = patch_shift[0]
    brick_ids = jnp.arange(bricks, dtype=jnp.int32)
    lane_ids = jnp.arange(4, dtype=jnp.int32)
    live_slots = slot_rank < all_rows
    dest_shard = slot_rank // shard_rows
    run_starts = jnp.sum(
        (slot_rank[:, None] < (brick_ids * shard_rows)[None, :]).astype(jnp.int32), axis=0
    )
    live_count = jnp.sum(live_slots.astype(jnp.int32))
    run_stops = jnp.concatenate([run_starts[1:], live_count[None]])
    source_brick = curve_order // capacity
    source_slot = curve_order % capacity
    source_lane = (source_brick - my_index + 1) % bricks
    from_lane = source_lane[:, None] == lane_ids[None, :]
    first_slot = jnp.min(jnp.where(from_lane, source_slot[:, None], capacity), axis=0)
    first_of_row = jnp.sum(jnp.where(from_lane, first_slot[None, :], 0), axis=1)
    recv_index = source_lane * pair_rows + source_slot - first_of_row
    column_start = lax.axis_index("mp") * width_part
    feature_part = lax.dynamic_slice_in_dim(voxel_feats, column_start, width_part, 1)
    lanes_in = []
    for lane in range(4):
        step = lane - 1
        target = (my_index - step) % bricks
        slots = run_starts[target] + jnp.arange(pair_rows, dtype=jnp.int32)
        valid = slots < run_stops[target]
        rows = feature_part[jnp.minimum(slots, capacity - 1)]
        piece = jnp.where(valid[:, None], rows, jnp.zeros_like(rows))
        if step != 0:
            piece = shifted(piece, "brick", -step)
        lanes_in.append(piece)
    local_part = jnp.concatenate(lanes_in, axis=0)[recv_index]
    local_rows = lax.all_gather(local_part, "mp", axis=1, tiled=True)
    head_next = shifted(local_rows[:PATCH], "brick", -1)
    window = lax.dynamic_slice_in_dim(
        jnp.concatenate([local_rows, head_next], axis=0), offset, shard_rows, 0
    )
    normed = layer_norm(window, norm_gains[0])
    qkv_rows = jnp.dot(normed, qkv_weight, preferred_element_type=jnp.float32).astype(jnp.bfloat16)
    heads_here = HEADS // model_parts
    attended = patch_attention(qkv_rows, heads_here, PATCH)
    head_partial = jnp.dot(attended, proj_weight, preferred_element_type=jnp.float32).astype(
        jnp.bfloat16
    )
    mixed = lax.psum(head_partial, "mp").astype(jnp.float32)
    hidden_state = (window.astype(jnp.float32) + mixed).astype(jnp.bfloat16)
    normed_two = layer_norm(hidden_state, norm_gains[1])
    expanded = jax.nn.gelu(
        jnp.dot(normed_two, up_weight, preferred_element_type=jnp.float32), approximate=False
    ).astype(jnp.bfloat16)
    mlp_terms = jnp.dot(expanded, down_weight, preferred_element_type=jnp.float32).astype(
        jnp.bfloat16
    )
    mlp_sum = lax.psum_scatter(mlp_terms, "mp", scatter_dimension=1, tiled=True).astype(jnp.float32)
    column_offset = lax.axis_index("mp") * mlp_sum.shape[1]
    hidden_part = lax.dynamic_slice_in_dim(hidden_state, column_offset, mlp_sum.shape[1], 1)
    result_window = (hidden_part.astype(jnp.float32) + mlp_sum).astype(jnp.bfloat16)
    tail_rows = shifted(result_window[shard_rows - PATCH :], "brick", 1)
    own_rows = lax.dynamic_slice_in_dim(
        jnp.concatenate([tail_rows, result_window], axis=0), PATCH - offset, shard_rows, 0
    )
    back_rows = (
        jnp.zeros((4 * pair_rows, own_rows.shape[1]), jnp.bfloat16).at[recv_index].set(own_rows)
    )
    back_rows = back_rows.reshape(4, pair_rows, own_rows.shape[1])
    lanes_out = []
    for lane in range(4):
        step = lane - 1
        piece = back_rows[lane]
        if step != 0:
            piece = shifted(piece, "brick", step)
        lanes_out.append(piece)
    returned = jnp.concatenate(lanes_out, axis=0)
    to_shard = dest_shard[:, None] == brick_ids[None, :]
    start_of_slot = jnp.sum(jnp.where(to_shard, run_starts[None, :], 0), axis=1)
    slot_ids = jnp.arange(capacity, dtype=jnp.int32)
    slot_lane = (my_index - dest_shard + 1) % bricks
    back_index = jnp.where(live_slots, slot_lane * pair_rows + slot_ids - start_of_slot, 0)
    picked = returned[back_index]
    return jnp.where(live_slots[:, None], picked, jnp.zeros_like(picked))


def solution(mesh):
    return jax.shard_map(
        per_device,
        mesh=mesh,
        in_specs=(
            P("brick", None),
            P("brick"),
            P("brick"),
            P(),
            P(None, "mp"),
            P("mp", None),
            P(None, "mp"),
            P("mp", None),
            P(),
        ),
        out_specs=P("brick", "mp"),
        check_vma=False,
    )
```

profile of v0, /device:TPU:0, one launch (start us, length us, event | category | flops | bytes accessed | tf_op | source)
XLA Modules:
  0.0 443.3 jit_solution(11269930382451343480)
XLA Ops:
  15.5 2.8 gather_fusion
  19.2 3.0 collective-permute-start
  24.0 2.8 gather_fusion.2
  27.7 3.0 collective-permute-start.1
  32.7 2.8 gather_fusion.3
  36.3 2.0 collective-permute-start.2
  40.3 2.8 gather_fusion.1
  44.2 2.0 pad_maximum_fusion
  46.2 8.9 %gather_fusion.4 = bf16[2048,128]{1,0:T(8,128)(2,1)} fusion(bf16[3072,128]{1,0:T(8,128)(2,1)} %pad_maximum_fusion, s32[2048]{0:T(1024)S(1)} %get-tuple-element.76), kind=kCustom, calls=%fused_computation.4 | custom fusion | bytes 1056768 | tf_op jit(solution)/shard_map/gather | solution.py:110
  55.1 22.0 %all-gather.3.cloned.1.call-done = bf16[2048,512]{1,0:T(8,128)(2,1)} async-done(((bf16[2048,128]{1,0:T(8,128)(2,1)}), bf16[2048,512]{1,0:T(8,128)(2,1)}) %all-gather.3.cloned.1.call-update) | async-done | bytes 2097168 | tf_op jit(solution)/shard_map/all_gather | solution.py:111
  77.1 2.3 slice.64
  79.4 4.2 collective-permute-start.3
  84.9 21.9 %collective-permute-done.3 = bf16[1024,512]{1,0:T(8,128)(2,1)} collective-permute-done((bf16[1024,512]{1,0:T(8,128)(2,1)}, bf16[1024,512]{1,0:T(8,128)(2,1)}, u32[]{:S(2)}, u32[]{:S(2)}) %collective-permute-start.3) | collective-permute-done | bytes 1048608 | tf_op jit(solution)/shard_map/ppermute | solution.py:18
  106.8 3.1 convert_reduce_fusion
  111.0 2.4 convolution_convert_fusion.2
  113.4 161.6 %while.21 = (s32[]{:T(128)}, bf16[2,1024,128]{2,1,0:T(8,128)(2,1)}, bf16[2,1024,384]{2,1,0:T(8,128)(2,1)}, s32[]{:T(128)}, s32[]{:T(128)}, /*index=5*/s32[]{:T(128)}) while((s32[]{:T(128)}, bf16[2,1024,128]{2,1,0:T(8,128)(2,1)}, bf16[2,1024,384]{2,1,0:T(8,128)(2,1)}, s32[]{:T(128)}, s32[]{:T(128)}, /*index=5*/s32[]{:T(128)}) %tuple.72), condition=%wide.region_11.12_spmd, body=%wide.region_6.11_spmd.sunk | while | flops 306255872 | bytes 72648360 | solution.py:57
  113.4 2.1 constant_dynamic-slice_fusion.6
  115.5 2.3 copy.34
  117.8 74.6 %while.22 = (s32[]{:T(128)}, bf16[2,1024,4,16]{1,3,2,0:T(8,128)(2,1)}, bf16[2,1024,4,3,16]{1,4,3,2,0:T(8,128)(2,1)}, s32[]{:T(128)}) while((s32[]{:T(128)}, bf16[2,1024,4,16]{1,3,2,0:T(8,128)(2,1)}, bf16[2,1024,4,3,16]{1,4,3,2,0:T(8,128)(2,1)}, s32[]{:T(128)}) %tuple.71), condition=%wide.region_10.10_spmd, body=%wide.region_7.9_spmd.sunk | while | flops 306255872 | bytes 68453432 | solution.py:53
  118.8 8.1 %fusion.121 = f32[4,1024,1024]{1,2,0:T(8,128)} fusion(bf16[1024,4,3,16]{0,3,1,2:T(8,128)(2,1)S(1)} %copy_bitcast_fusion.2), kind=kOutput, calls=%fused_computation.19.clone.1 | convolution fusion | flops 134217728 | bytes 17039360 | tf_op jit(solution)/shard_map/while/body/eval_jaxpr/while/body/eval_jaxpr/qhd,khd->hqk/dot_general | solution.py:37
  126.9 12.6 %fusion.122 = f32[4,1024]{1,0:T(4,128)S(1)} fusion(f32[4,1024,1024]{1,2,0:T(8,128)} %fusion.121), kind=kOutput, calls=%fused_computation.180.clone.1 | output fusion | flops 16778240 | bytes 16793600 | tf_op jit(solution)/shard_map/while/body/eval_jaxpr/while/body/eval_jaxpr/sub | solution.py:43
  139.5 15.6 %fusion.123 = bf16[2,1024,4,16]{1,3,2,0:T(8,128)(2,1)} fusion(bf16[2,1024,4,16]{1,3,2,0:T(8,128)(2,1)} %get-tuple-element.150, s32[]{:T(128)} %get-tuple-element.149, f32[4,1024]{1,0:T(4,128)S(1)} %fusion.122, bf16[1024,4,3,16]{0,3,1,2:T(8,128)(2,1)S(1)} %copy_bitcast_fusion.2, f32[4,1024,1024]{1,2,0:T(8,128)} %fusion.121), kind=kOutput, calls=%fused_computation.16.clone.1 | convolution fusion | flops 155259904 | bytes 33833472 | tf_op jit(solution)/shard_map/while/body/eval_jaxpr/while/body/eval_jaxpr/hqk,khd->qhd/dot_general | solution.py:47
  156.1 8.1 %fusion.121 = f32[4,1024,1024]{1,2,0:T(8,128)} fusion(bf16[1024,4,3,16]{0,3,1,2:T(8,128)(2,1)S(1)} %copy_bitcast_fusion.2), kind=kOutput, calls=%fused_computation.19.clone.1 | convolution fusion | flops 134217728 | bytes 17039360 | tf_op jit(solution)/shard_map/while/body/eval_jaxpr/while/body/eval_jaxpr/qhd,khd->hqk/dot_general | solution.py:37
  164.2 12.6 %fusion.122 = f32[4,1024]{1,0:T(4,128)S(1)} fusion(f32[4,1024,1024]{1,2,0:T(8,128)} %fusion.121), kind=kOutput, calls=%fused_computation.180.clone.1 | output fusion | flops 16778240 | bytes 16793600 | tf_op jit(solution)/shard_map/while/body/eval_jaxpr/while/body/eval_jaxpr/sub | solution.py:43
  176.8 15.6 %fusion.123 = bf16[2,1024,4,16]{1,3,2,0:T(8,128)(2,1)} fusion(bf16[2,1024,4,16]{1,3,2,0:T(8,128)(2,1)} %get-tuple-element.150, s32[]{:T(128)} %get-tuple-element.149, f32[4,1024]{1,0:T(4,128)S(1)} %fusion.122, bf16[1024,4,3,16]{0,3,1,2:T(8,128)(2,1)S(1)} %copy_bitcast_fusion.2, f32[4,1024,1024]{1,2,0:T(8,128)} %fusion.121), kind=kOutput, calls=%fused_computation.16.clone.1 | convolution fusion | flops 155259904 | bytes 33833472 | tf_op jit(solution)/shard_map/while/body/eval_jaxpr/while/body/eval_jaxpr/hqk,khd->qhd/dot_general | solution.py:47
  194.2 2.1 constant_dynamic-slice_fusion.6
  196.3 2.3 copy.34
  198.6 74.6 %while.22 = (s32[]{:T(128)}, bf16[2,1024,4,16]{1,3,2,0:T(8,128)(2,1)}, bf16[2,1024,4,3,16]{1,4,3,2,0:T(8,128)(2,1)}, s32[]{:T(128)}) while((s32[]{:T(128)}, bf16[2,1024,4,16]{1,3,2,0:T(8,128)(2,1)}, bf16[2,1024,4,3,16]{1,4,3,2,0:T(8,128)(2,1)}, s32[]{:T(128)}) %tuple.71), condition=%wide.region_10.10_spmd, body=%wide.region_7.9_spmd.sunk | while | flops 306255872 | bytes 68453432 | solution.py:53
  199.6 8.1 %fusion.121 = f32[4,1024,1024]{1,2,0:T(8,128)} fusion(bf16[1024,4,3,16]{0,3,1,2:T(8,128)(2,1)S(1)} %copy_bitcast_fusion.2), kind=kOutput, calls=%fused_computation.19.clone.1 | convolution fusion | flops 134217728 | bytes 17039360 | tf_op jit(solution)/shard_map/while/body/eval_jaxpr/while/body/eval_jaxpr/qhd,khd->hqk/dot_general | solution.py:37
  207.7 12.6 %fusion.122 = f32[4,1024]{1,0:T(4,128)S(1)} fusion(f32[4,1024,1024]{1,2,0:T(8,128)} %fusion.121), kind=kOutput, calls=%fused_computation.180.clone.1 | output fusion | flops 16778240 | bytes 16793600 | tf_op jit(solution)/shard_map/while/body/eval_jaxpr/while/body/eval_jaxpr/sub | solution.py:43
  220.3 15.6 %fusion.123 = bf16[2,1024,4,16]{1,3,2,0:T(8,128)(2,1)} fusion(bf16[2,1024,4,16]{1,3,2,0:T(8,128)(2,1)} %get-tuple-element.150, s32[]{:T(128)} %get-tuple-element.149, f32[4,1024]{1,0:T(4,128)S(1)} %fusion.122, bf16[1024,4,3,16]{0,3,1,2:T(8,128)(2,1)S(1)} %copy_bitcast_fusion.2, f32[4,1024,1024]{1,2,0:T(8,128)} %fusion.121), kind=kOutput, calls=%fused_computation.16.clone.1 | convolution fusion | flops 155259904 | bytes 33833472 | tf_op jit(solution)/shard_map/while/body/eval_jaxpr/while/body/eval_jaxpr/hqk,khd->qhd/dot_general | solution.py:47
  236.9 8.1 %fusion.121 = f32[4,1024,1024]{1,2,0:T(8,128)} fusion(bf16[1024,4,3,16]{0,3,1,2:T(8,128)(2,1)S(1)} %copy_bitcast_fusion.2), kind=kOutput, calls=%fused_computation.19.clone.1 | convolution fusion | flops 134217728 | bytes 17039360 | tf_op jit(solution)/shard_map/while/body/eval_jaxpr/while/body/eval_jaxpr/qhd,khd->hqk/dot_general | solution.py:37
  245.0 12.6 %fusion.122 = f32[4,1024]{1,0:T(4,128)S(1)} fusion(f32[4,1024,1024]{1,2,0:T(8,128)} %fusion.121), kind=kOutput, calls=%fused_computation.180.clone.1 | output fusion | flops 16778240 | bytes 16793600 | tf_op jit(solution)/shard_map/while/body/eval_jaxpr/while/body/eval_jaxpr/sub | solution.py:43
  257.6 15.6 %fusion.123 = bf16[2,1024,4,16]{1,3,2,0:T(8,128)(2,1)} fusion(bf16[2,1024,4,16]{1,3,2,0:T(8,128)(2,1)} %get-tuple-element.150, s32[]{:T(128)} %get-tuple-element.149, f32[4,1024]{1,0:T(4,128)S(1)} %fusion.122, bf16[1024,4,3,16]{0,3,1,2:T(8,128)(2,1)S(1)} %copy_bitcast_fusion.2, f32[4,1024,1024]{1,2,0:T(8,128)} %fusion.121), kind=kOutput, calls=%fused_computation.16.clone.1 | convolution fusion | flops 155259904 | bytes 33833472 | tf_op jit(solution)/shard_map/while/body/eval_jaxpr/while/body/eval_jaxpr/hqk,khd->qhd/dot_general | solution.py:47
  275.0 3.0 convolution_convert_fusion
  278.3 52.2 %all-reduce.2.cloned.1.call-done = bf16[2048,512]{1,0:T(8,128)(2,1)} async-done(((bf16[2048,512]{1,0:T(8,128)(2,1)}), bf16[2048,512]{1,0:T(8,128)(2,1)}) %all-reduce.2.cloned.1.call-update) | async-done | bytes 2097168 | tf_op jit(solution)/shard_map/psum | solution.py:123
  330.5 2.9 convert_reduce_fusion.1
  335.8 13.2 %convolution_convert_fusion.1 = bf16[2048,512]{1,0:T(8,128)(2,1)} fusion(bf16[512,512]{1,0:T(8,128)(2,1)} %param.20, bf16[512,512]{1,0:T(8,128)(2,1)} %param.19, bf16[2048,512]{1,0:T(8,128)(2,1)} %copy-done.2, f32[512]{0:T(512)S(1)} %bitcast.69, f32[2048]{0:T(1024)S(1)} %add_rsqrt_fusion, f32[2048]{0:T(1024)S(1)} %broadcast_multiply_fusion), kind=kOutput, calls=%fused_computation.66 | convolution fusion | flops 2221932544 | bytes 5261312 | tf_op jit(solution)/shard_map/dot_general | solution.py:129
  349.1 4.0 copy.24
  353.1 31.6 %reduce-scatter.4.cloned.1.call-done = bf16[128,2048]{1,0:T(8,128)(2,1)} async-done(((bf16[512,2048]{1,0:T(8,128)(2,1)}), bf16[128,2048]{1,0:T(8,128)(2,1)}) %reduce-scatter.4.cloned.1.call-update) | async-done | bytes 524304
  384.7 2.0 copy.25
  390.4 9.4 %collective-permute-done.4 = bf16[1024,128]{1,0:T(8,128)(2,1)} collective-permute-done((bf16[1024,128]{1,0:T(8,128)(2,1)S(1)}, bf16[1024,128]{1,0:T(8,128)(2,1)}, u32[]{:S(2)}, u32[]{:S(2)}) %collective-permute-start.4) | collective-permute-done | bytes 262176 | tf_op jit(solution)/shard_map/ppermute | solution.py:18
  399.8 7.5 %scatter_custom_fusion = bf16[3072,128]{1,0:T(8,128)(2,1)} fusion(s32[2048]{0:T(1024)} %get-tuple-element.77, s32[]{:T(128)S(6)} %select_n.175, s32[]{:T(128)} %constant.86.clone.1, bf16[1024,128]{1,0:T(8,128)(2,1)} %collective-permute-done.4, bf16[]{:T(256)} %constant.218, bf16[2048,128]{1,0:T(8,128)(2,1)} %copy-done.3, bf16[]{:T(256)} %constant.82.clone.1), kind=kCustom, calls=%fused_computation.83 | custom fusion | flops 1048576 | bytes 1574404 | tf_op jit(solution)/shard_map/scatter | solution.py:141
  408.5 1.6 collective-permute-start.5
  410.6 5.8 %collective-permute-done.5 = bf16[768,128]{1,0:T(8,128)(2,1)S(1)} collective-permute-done((bf16[768,128]{1,0:T(8,128)(2,1)S(1)}, bf16[768,128]{1,0:T(8,128)(2,1)S(1)}, u32[]{:S(2)}, u32[]{:S(2)}) %collective-permute-start.5) | collective-permute-done | bytes 196640 | tf_op jit(solution)/shard_map/ppermute | solution.py:18
  416.4 4.0 collective-permute-done.6
  421.4 12.1 %gather_fusion.5 = bf16[3072,128]{1,0:T(8,128)(2,1)} fusion(bf16[3072,128]{1,0:T(8,128)(2,1)} %pad_maximum_fusion.1, s32[3072]{0:T(1024)S(1)} %copy-done.4), kind=kCustom, calls=%fused_computation.5 | custom fusion | bytes 1585152 | tf_op jit(solution)/shard_map/gather | solution.py:157
  433.5 3.3 broadcast_select_fusion
  (87 shorter events, 36.7 us)
Async XLA Ops:
  6.5 7.9 %copy-start = (bf16[3072,512]{1,0:T(8,128)(2,1)S(1)}, bf16[3072,512]{1,0:T(8,128)(2,1)}, u32[]{:S(2)}) copy-start(bf16[3072,512]{1,0:T(8,128)(2,1)} %param.13) | copy-start | bytes 9437188
  6.5 70.5 %all-gather.3.cloned.1.call-start = ((), (), s32[]{:S(2)}) async-start(), calls=%async_computation.2 | async-start | bytes 2621440 | tf_op jit(solution)/shard_map/all_gather | solution.py:111
  9.9 0.6 copy-start.6
  15.5 27.7 %copy-start.5 = (s32[2048]{0:T(1024)S(1)}, s32[2048]{0:T(1024)}, u32[]{:S(2)}) copy-start(s32[2048]{0:T(1024)} %param.15) | copy-start | bytes 24580
  19.2 25.0 %collective-permute-start = (bf16[768,128]{1,0:T(8,128)(2,1)}, bf16[768,128]{1,0:T(8,128)(2,1)S(1)}, u32[]{:S(2)}, u32[]{:S(2)}) collective-permute-start(bf16[768,128]{1,0:T(8,128)(2,1)} %broadcast_select_fusion.4), channel_id=1, source_target_pairs={{0,4},{4,8},{8,12},{12,16},{16,20},{20,24},{24,28},{28,0},{1,5},{5... | collective-permute-start | bytes 589832 | tf_op jit(solution)/shard_map/ppermute | solution.py:18
  27.7 16.5 %collective-permute-start.1 = (bf16[768,128]{1,0:T(8,128)(2,1)}, bf16[768,128]{1,0:T(8,128)(2,1)}, u32[]{:S(2)}, u32[]{:S(2)}) collective-permute-start(bf16[768,128]{1,0:T(8,128)(2,1)} %broadcast_select_fusion.2), channel_id=1, source_target_pairs={{0,28},{4,0},{8,4},{12,8},{16,12},{20,16},{24,20},{28,24},{1,29},{... | collective-permute-start | bytes 589832 | tf_op jit(solution)/shard_map/ppermute | solution.py:18
  36.3 7.9 %collective-permute-start.2 = (bf16[768,128]{1,0:T(8,128)(2,1)}, bf16[768,128]{1,0:T(8,128)(2,1)}, u32[]{:S(2)}, u32[]{:S(2)}) collective-permute-start(bf16[768,128]{1,0:T(8,128)(2,1)} %broadcast_select_fusion.1), channel_id=1, source_target_pairs={{0,24},{4,28},{8,0},{12,4},{16,8},{20,12},{24,16},{28,20},{1,25},{... | collective-permute-start | bytes 589832 | tf_op jit(solution)/shard_map/ppermute | solution.py:18
  44.2 40.0 %copy-start.8 = (f32[2,512]{1,0:T(2,128)S(1)}, f32[2,512]{1,0:T(2,128)}, u32[]{:S(2)}) copy-start(f32[2,512]{1,0:T(2,128)} %param.21) | copy-start | bytes 12292
  55.1 275.5 %all-reduce.2.cloned.1.call-start = ((), (), s32[]{:S(2)}) async-start(), calls=%async_computation.1 | async-start | bytes 4194304 | tf_op jit(solution)/shard_map/psum | solution.py:123
  79.4 31.6 %copy-start.10 = (bf16[512,384]{1,0:T(8,128)(2,1)S(1)}, bf16[512,384]{1,0:T(8,128)(2,1)}, u32[]{:S(2)}) copy-start(bf16[512,384]{1,0:T(8,128)(2,1)} %param.17) | copy-start | bytes 1179652
  79.4 27.4 %collective-permute-start.3 = (bf16[1024,512]{1,0:T(8,128)(2,1)}, bf16[1024,512]{1,0:T(8,128)(2,1)}, u32[]{:S(2)}, u32[]{:S(2)}) collective-permute-start(bf16[1024,512]{1,0:T(8,128)(2,1)} %slice.64), channel_id=1, source_target_pairs={{0,28},{4,0},{8,4},{12,8},{16,12},{20,16},{24,20},{28,24},{1,29},{... | collective-permute-start | bytes 3145736 | tf_op jit(solution)/shard_map/ppermute | solution.py:18
  109.9 3.5 copy-start.1
  278.1 57.8 %copy-start.9 = (f32[1,512]{1,0:T(1,128)S(1)}, f32[1,512]{1,0:T(1,128)}, u32[]{:S(2)}) copy-start(f32[1,512]{1,0:T(1,128)} %get-tuple-element.84) | copy-start | bytes 6148
  278.1 106.6 %reduce-scatter.4.cloned.1.call-start = ((), (), s32[]{:S(2)}) async-start(), calls=%async_computation.3 | async-start | bytes 2621440
  333.4 1.4 copy-start.2
  353.0 68.3 %copy-start.4 = (s32[3072]{0:T(1024)S(1)}, s32[3072]{0:T(1024)}, u32[]{:S(2)}) copy-start(s32[3072]{0:T(1024)} %get-tuple-element.70) | copy-start | bytes 36868
  388.1 0.8 copy-start.3
  388.9 10.9 %collective-permute-start.4 = (bf16[1024,128]{1,0:T(8,128)(2,1)S(1)}, bf16[1024,128]{1,0:T(8,128)(2,1)}, u32[]{:S(2)}, u32[]{:S(2)}) collective-permute-start(bf16[1024,128]{1,0:T(8,128)(2,1)S(1)} %slice.65), channel_id=1, source_target_pairs={{0,4},{4,8},{8,12},{12,16},{16,20},{20,24},{24,28},{28,0},{1,5},{5... | collective-permute-start | bytes 786440 | tf_op jit(solution)/shard_map/ppermute | solution.py:18
  408.5 7.9 %collective-permute-start.5 = (bf16[768,128]{1,0:T(8,128)(2,1)S(1)}, bf16[768,128]{1,0:T(8,128)(2,1)S(1)}, u32[]{:S(2)}, u32[]{:S(2)}) collective-permute-start(bf16[768,128]{1,0:T(8,128)(2,1)S(1)} %get-tuple-element.78), channel_id=1, source_target_pairs={{0,28},{4,0},{8,4},{12,8},{16,12},{20,16},{24,20},{28,24},{1,29},{... | collective-permute-start | bytes 589832 | tf_op jit(solution)/shard_map/ppermute | solution.py:18
  410.1 10.3 %collective-permute-start.6 = (bf16[768,128]{1,0:T(8,128)(2,1)S(1)}, bf16[768,128]{1,0:T(8,128)(2,1)S(1)}, u32[]{:S(2)}, u32[]{:S(2)}) collective-permute-start(bf16[768,128]{1,0:T(8,128)(2,1)S(1)} %get-tuple-element.80), channel_id=1, source_target_pairs={{0,4},{4,8},{8,12},{12,16},{16,20},{20,24},{24,28},{28,0},{1,5},{5... | collective-permute-start | bytes 589832 | tf_op jit(solution)/shard_map/ppermute | solution.py:18
  410.6 9.8 %collective-permute-start.7 = (bf16[768,128]{1,0:T(8,128)(2,1)S(1)}, bf16[768,128]{1,0:T(8,128)(2,1)S(1)}, u32[]{:S(2)}, u32[]{:S(2)}) collective-permute-start(bf16[768,128]{1,0:T(8,128)(2,1)S(1)} %get-tuple-element.79), channel_id=1, source_target_pairs={{0,8},{4,12},{8,16},{12,20},{16,24},{20,28},{24,0},{28,4},{1,9},{5... | collective-permute-start | bytes 589832 | tf_op jit(solution)/shard_map/ppermute | solution.py:18
  420.4 13.1 %copy-start.7 = (pred[3072]{0:T(1024)(128)(4,1)S(1)}, pred[3072]{0:T(1024)(128)(4,1)}, u32[]{:S(2)}) copy-start(pred[3072]{0:T(1024)(128)(4,1)} %copy-done.6) | copy-start | bytes 9220
Sparse Core Ops, SparseCore 0:
  55.2 21.8 all-gather.2
  278.2 52.3 all-reduce.1
  353.2 31.4 reduce-scatter.3
where the time goes:
time: 445 us; the launch traced here: 443 us
  waiting for transfers between devices  147 us (33%)
  matrix products  113 us (25%)
  other arithmetic  89.3 us (20%)
  local copies, waits for them, and re-layouts  63.5 us (14%)
  starting transfers between devices  16.1 us (4%)
  between operations  14.1 us (3%)
    dot_general x4, matrix products, one_group(): jnp.einsum('hqk,khd->qhd', softmax_weights, piece[:, :, 2], preferred_ele...  62.3 us
    psum x1, waiting for transfers between devices, per_device(): mixed = lax.psum(head_partial, 'mp').astype(jnp.float32)  52.2 us
    sub x4, other arithmetic, one_group(): weights_exp = jnp.exp(scores - highest)  50.3 us
    ppermute x8, waiting for transfers between devices, shifted(): return lax.ppermute(value, axis, pairs)  41.1 us
    dot_general x4, matrix products, one_group(): jnp.einsum('qhd,khd->hqk', piece[:, :, 0], piece[:, :, 1], preferred_elem...  32.4 us
    unnamed x4, waiting for transfers between devices  31.7 us
    all_gather x1, waiting for transfers between devices, per_device(): local_rows = lax.all_gather(local_part, 'mp', axis=1, tiled=True)  22 us
    ppermute x8, starting transfers between devices, shifted(): return lax.ppermute(value, axis, pairs)  15.8 us
  transfers between devices with their start and end apart: 11, of which 7 were waited for; matrix products, arithmetic and copies ran while one was open for 4% of the time, Pallas kernels for 0%

commit v1 on v0

v1 whole, which is shorter than its diff:
```python
import functools
import math

import jax
import jax.numpy as jnp
from jax import lax
from jax.experimental import pallas as pl
from jax.experimental.pallas import tpu as pltpu
from jax.sharding import PartitionSpec as P

HEADS = 32
PATCH = 1024
EPSILON = 1e-05
VMEM_BYTES = 56 * 1024 * 1024


def shifted(value, axis, steps):
    count = lax.axis_size(axis)
    pairs = [(source, (source + steps) % count) for source in range(count)]
    return lax.ppermute(value, axis, pairs)


def layer_norm(values, gain):
    centred = values - jnp.mean(values, axis=-1, keepdims=True)
    spread = jnp.mean(centred * centred, axis=-1, keepdims=True)
    return (centred * lax.rsqrt(spread + EPSILON) * gain).astype(jnp.bfloat16)


def attention_kernel(
    head_dim,
    query_tile,
    query_from,
    patch_rows,
    gain,
    weights,
    attended,
    normed,
    queries,
    keys,
    values,
):
    groups, _, triple = weights.shape
    lanes = triple // 3
    group_heads = lanes // head_dim
    query_rows = attended.shape[0]
    normed[...] = layer_norm(patch_rows[...].astype(jnp.float32), gain[...])
    start = pl.multiple_of(query_from[0], query_rows)
    scale = head_dim ** (-0.5) * math.log2(math.e)
    lane_head = lax.broadcasted_iota(jnp.int32, (1, lanes), 1) // head_dim
    for group in range(groups):
        weight = weights[group]
        queries[group] = (
            jnp.dot(
                normed[pl.ds(start, query_rows), :],
                weight[:, :lanes],
                preferred_element_type=jnp.float32,
            )
            * scale
        ).astype(jnp.bfloat16)
        both = jnp.dot(
            normed[...], weight[:, lanes:], preferred_element_type=jnp.float32
        ).astype(jnp.bfloat16)
        keys[group] = both[:, :lanes]
        values[group, :, :lanes] = both[:, lanes:]
        values[group, :, lanes:] = jnp.ones_like(both[:, lanes:])

    def one_group(group, carry):
        attended_group = [
            jnp.zeros((query_tile, lanes), jnp.float32)
            for _ in range(query_rows // query_tile)
        ]

        def one_head(head, sums):
            mine = lane_head == head
            results = []
            for tile in range(query_rows // query_tile):
                query = queries[group, tile * query_tile : (tile + 1) * query_tile, :]
                query = jnp.where(mine, query, jnp.zeros_like(query))
                scores = lax.dot_general(
                    query,
                    keys[group],
                    (((1,), (1,)), ((), ())),
                    preferred_element_type=jnp.float32,
                )
                highest = jnp.max(scores, axis=-1, keepdims=True)
                exps = jnp.exp2(scores - highest).astype(jnp.bfloat16)
                product = jnp.dot(
                    exps, values[group], preferred_element_type=jnp.float32
                )
                result = product[:, :lanes] / product[:, lanes:]
                results.append(jnp.where(mine, result, sums[tile]))
            return tuple(results)

        sums = lax.fori_loop(0, group_heads, one_head, tuple(attended_group))
        for tile in range(query_rows // query_tile):
            attended[tile * query_tile : (tile + 1) * query_tile, pl.ds(
                pl.multiple_of(group * lanes, lanes), lanes
            )] = sums[tile].astype(jnp.bfloat16)
        return carry

    lax.fori_loop(0, groups, one_group, 0)


def attention(patch_rows, gain, weights, query_from, query_rows, head_dim):
    groups, width, triple = weights.shape
    lanes = triple // 3
    rows = patch_rows.shape[0]
    whole = pl.BlockSpec(memory_space=pltpu.VMEM)
    return pl.pallas_call(
        functools.partial(attention_kernel, head_dim, query_rows // 4),
        out_shape=jax.ShapeDtypeStruct((query_rows, groups * lanes), jnp.bfloat16),
        in_specs=[pl.BlockSpec(memory_space=pltpu.SMEM), whole, whole, whole],
        out_specs=whole,
        scratch_shapes=[
            pltpu.VMEM((rows, width), jnp.bfloat16),
            pltpu.VMEM((groups, query_rows, lanes), jnp.bfloat16),
            pltpu.VMEM((groups, rows, lanes), jnp.bfloat16),
            pltpu.VMEM((groups, rows, 2 * lanes), jnp.bfloat16),
        ],
        compiler_params=pltpu.CompilerParams(vmem_limit_bytes=VMEM_BYTES),
        cost_estimate=pl.CostEstimate(
            flops=4 * rows * query_rows * groups * lanes * 16,
            bytes_accessed=4 * rows * width,
            transcendentals=rows * query_rows * groups * 8,
        ),
    )(query_from, patch_rows, gain, weights)


def mlp_kernel(
    query_from, patch_rows, attended, gain, proj_weight, up_weight, down_weight, result
):
    groups, depth, _ = proj_weight.shape
    rows = attended.shape[0]
    start = pl.multiple_of(query_from[0], rows)
    own = patch_rows[pl.ds(start, rows), :].astype(jnp.float32)
    mixed = None
    for group in range(groups):
        term = jnp.dot(
            attended[:, group * depth : (group + 1) * depth],
            proj_weight[group],
            preferred_element_type=jnp.float32,
        ).astype(jnp.bfloat16).astype(jnp.float32)
        mixed = term if mixed is None else mixed + term
    hidden = (own + mixed).astype(jnp.bfloat16).astype(jnp.float32)
    normed = layer_norm(hidden, gain[...])
    total = None
    for group in range(groups):
        expanded = jnp.dot(normed, up_weight[group], preferred_element_type=jnp.float32)
        expanded = (
            0.5 * expanded * (1.0 + lax.erf(expanded * math.sqrt(0.5)))
        ).astype(jnp.bfloat16)
        term = jnp.dot(
            expanded, down_weight[group], preferred_element_type=jnp.float32
        ).astype(jnp.bfloat16).astype(jnp.float32)
        total = term if total is None else total + term
    result[...] = (hidden + total).astype(jnp.bfloat16)


def mlp(patch_rows, attended, gain, proj_weight, up_weight, down_weight, query_from):
    whole = pl.BlockSpec(memory_space=pltpu.VMEM)
    rows, width = attended.shape
    groups, _, hidden = up_weight.shape
    return pl.pallas_call(
        mlp_kernel,
        out_shape=jax.ShapeDtypeStruct(attended.shape, jnp.bfloat16),
        in_specs=[pl.BlockSpec(memory_space=pltpu.SMEM)] + [whole] * 6,
        out_specs=whole,
        compiler_params=pltpu.CompilerParams(vmem_limit_bytes=VMEM_BYTES),
        cost_estimate=pl.CostEstimate(
            flops=4 * rows * width * hidden * groups,
            bytes_accessed=8 * width * hidden * groups,
            transcendentals=rows * hidden * groups,
        ),
    )(query_from, patch_rows, attended, gain, proj_weight, up_weight, down_weight)


def per_device(
    voxel_feats,
    slot_rank,
    curve_order,
    patch_shift,
    qkv_weight,
    proj_weight,
    up_weight,
    down_weight,
    norm_gains,
):
    bricks = lax.axis_size("brick")
    model_parts = lax.axis_size("mp")
    my_index = lax.axis_index("brick")
    part_index = lax.axis_index("mp")
    capacity = voxel_feats.shape[0]
    shard_rows = curve_order.shape[0]
    pair_rows = 3 * (shard_rows // 8)
    width_full = voxel_feats.shape[1]
    width_part = width_full // model_parts
    quarter_rows = shard_rows // model_parts
    head_dim = width_full // HEADS
    offset = patch_shift[0]
    latest = capacity - pair_rows

    triple = qkv_weight.shape[1]
    spot = jnp.arange(triple, dtype=jnp.int32)
    kind, within = spot // width_part, spot % width_part
    origin = (within // head_dim) * 3 * head_dim + kind * head_dim + within % head_dim
    shuffle = (spot[:, None] == origin[None, :]).astype(jnp.bfloat16)
    qkv_sorted = jnp.dot(
        qkv_weight, shuffle, preferred_element_type=jnp.float32
    ).astype(jnp.bfloat16)
    qkv_all = lax.all_gather(qkv_sorted, "mp", axis=0)
    proj_all = lax.all_gather(proj_weight, "mp", axis=0)
    up_all = lax.all_gather(up_weight, "mp", axis=0)
    down_all = lax.all_gather(down_weight, "mp", axis=0)

    lane_ids = jnp.arange(4, dtype=jnp.int32)
    lane_targets = (my_index - (lane_ids - 1)) % bricks
    run_starts = jnp.sum(
        (slot_rank[:, None] < (lane_targets * shard_rows)[None, :]).astype(jnp.int32), axis=0
    )
    slab_starts = jnp.minimum(run_starts, latest)
    source_brick = curve_order // capacity
    source_slot = curve_order % capacity
    source_lane = (source_brick - my_index + 1) % bricks
    from_lane = source_lane[:, None] == lane_ids[None, :]
    first_slot = jnp.min(jnp.where(from_lane, source_slot[:, None], capacity), axis=0)
    first_slot = jnp.minimum(first_slot, latest)
    first_of_row = jnp.sum(jnp.where(from_lane, first_slot[None, :], 0), axis=1)
    recv_index = source_lane * pair_rows + source_slot - first_of_row
    select = (
        recv_index[:, None] == jnp.arange(4 * pair_rows, dtype=jnp.int32)[None, :]
    ).astype(jnp.bfloat16)

    lanes_in = []
    for lane in range(4):
        piece = lax.dynamic_slice(
            voxel_feats,
            (slab_starts[lane], part_index * width_part),
            (pair_rows, width_part),
        )
        if lane != 1:
            piece = shifted(piece, "brick", 1 - lane)
        lanes_in.append(piece)
    local_part = jnp.dot(
        select, jnp.concatenate(lanes_in, axis=0), preferred_element_type=jnp.float32
    ).astype(jnp.bfloat16)
    head_next = shifted(local_part[:PATCH], "brick", -1)
    window = lax.dynamic_slice_in_dim(
        jnp.concatenate([local_part, head_next], axis=0), offset, shard_rows, 0
    )

    def patch_of(part):
        return (part * quarter_rows) // PATCH

    pieces = []
    for step in range(model_parts):
        target = (part_index + step) % model_parts
        piece = lax.dynamic_slice_in_dim(window, patch_of(target) * PATCH, PATCH, 0)
        if step:
            piece = shifted(piece, "mp", step)
        pieces.append(piece)
    patch_rows = jnp.zeros((PATCH, width_full), jnp.bfloat16)
    for step in range(model_parts):
        source = (part_index - step) % model_parts
        patch_rows = lax.dynamic_update_slice_in_dim(
            patch_rows, pieces[step], source * width_part, 1
        )
    query_from = ((part_index * quarter_rows) % PATCH)[None]
    attended = attention(
        patch_rows, norm_gains[0:1], qkv_all, query_from, quarter_rows, head_dim
    )
    result = mlp(
        patch_rows, attended, norm_gains[1:2], proj_all, up_all, down_all, query_from
    )

    result_window = jnp.zeros((shard_rows, width_part), jnp.bfloat16)
    for step in range(model_parts):
        target = (part_index + step) % model_parts
        piece = lax.dynamic_slice_in_dim(result, target * width_part, width_part, 1)
        if step:
            piece = shifted(piece, "mp", step)
        source = (part_index - step) % model_parts
        result_window = lax.dynamic_update_slice_in_dim(
            result_window, piece, source * quarter_rows, 0
        )
    tail_rows = shifted(result_window[shard_rows - PATCH :], "brick", 1)
    own_rows = lax.dynamic_slice_in_dim(
        jnp.concatenate([tail_rows, result_window], axis=0), PATCH - offset, shard_rows, 0
    )
    back_rows = lax.dot_general(
        select, own_rows, (((0,), (0,)), ((), ())), preferred_element_type=jnp.float32
    ).astype(jnp.bfloat16)
    out = jnp.zeros((capacity, width_part), jnp.bfloat16)
    for lane in range(4):
        piece = back_rows[lane * pair_rows : (lane + 1) * pair_rows]
        if lane != 1:
            piece = shifted(piece, "brick", lane - 1)
        before = lax.dynamic_slice_in_dim(out, slab_starts[lane], pair_rows, 0)
        out = lax.dynamic_update_slice_in_dim(out, before + piece, slab_starts[lane], 0)
    return out


def solution(mesh):
    return jax.shard_map(
        per_device,
        mesh=mesh,
        in_specs=(
            P("brick", None),
            P("brick"),
            P("brick"),
            P(),
            P(None, "mp"),
            P("mp", None),
            P(None, "mp"),
            P("mp", None),
            P(),
        ),
        out_specs=P("brick", "mp"),
        check_vma=False,
    )
```

time: 445 us -> 179 us (0.40)
  waiting for transfers between devices: 147 us -> 39 us
  matrix products: 113 us -> 13.2 us
  other arithmetic: 89.3 us -> 5.49 us
  local copies, waits for them, and re-layouts: 63.5 us -> 13.5 us
  Pallas kernels: 0 us -> 45.8 us
  blocking collectives: 0 us -> 17.1 us
  between operations: 14.1 us -> 21.5 us
  starting transfers between devices: 16.1 us -> 23.2 us
    dot_general x11 -> x3, matrix products: 113 us -> 13.2 us  [the longest x1 7.58 us: per_device(): lax.dot_general(select, own_rows, (((0,), (0,)), ((), ())), preferred_ele...]
    psum x1 -> x0, waiting for transfers between devices: 52.2 us -> none  [per_device(): mixed = lax.psum(head_partial, 'mp').astype(jnp.float32)]
    sub x4 -> x1, other arithmetic: 50.3 us -> 0.02 us  [per_device(): recv_index = source_lane * pair_rows + source_slot - first_of_row]
    pallas_call x0 -> x2, Pallas kernels: none -> 45.8 us  [the longest x1 38.7 us: attention(): pl.pallas_call(functools.partial(attention_kernel, head_dim, query_rows /...]
    gather x6 -> x0, local copies, waits for them, and re-layouts: 32.3 us -> none  [the longest x1 12.1 us: per_device(): picked = returned[back_index]]
    unnamed x4 -> x3, waiting for transfers between devices: 31.7 us -> 0.73 us
    all_gather x1 -> x3, waiting for transfers between devices: 22 us -> 0.02 us  [the longest x1 0.02 us: per_device(): qkv_all = lax.all_gather(qkv_sorted, 'mp', axis=0)]
    all_gather x0 -> x1, blocking collectives: none -> 17.1 us  [per_device(): proj_all = lax.all_gather(proj_weight, 'mp', axis=0)]
  transfers between devices with their start and end apart: 11 -> 17, of which waited for: 7 -> 10; matrix products, arithmetic and copies ran while one was open for 4% -> 10% of each run, Pallas kernels for 0% -> 22%
where the time goes in v1:
time: 179 us
  Pallas kernels  45.8 us (26%)
  waiting for transfers between devices  39 us (22%)
  starting transfers between devices  23.2 us (13%)
  between operations  21.5 us (12%)
  blocking collectives  17.1 us (10%)
  local copies, waits for them, and re-layouts  13.5 us (8%)
  matrix products  13.2 us (7%)
  other arithmetic  5.49 us (3%)
    pallas_call x1, Pallas kernels, attention(): pl.pallas_call(functools.partial(attention_kernel, head_dim, query_rows /...  38.7 us
    ppermute x14, waiting for transfers between devices, shifted(): return lax.ppermute(value, axis, pairs)  38.2 us
    ppermute x14, starting transfers between devices, shifted(): return lax.ppermute(value, axis, pairs)  23.1 us
    all_gather x1, blocking collectives, per_device(): proj_all = lax.all_gather(proj_weight, 'mp', axis=0)  17.1 us
    dot_general x1, matrix products, per_device(): lax.dot_general(select, own_rows, (((0,), (0,)), ((), ())), preferred_ele...  7.58 us
    pallas_call x1, Pallas kernels, mlp(): pl.pallas_call(mlp_kernel, out_shape=jax.ShapeDtypeStruct(attended.shape,...  7.04 us
    dot_general x1, matrix products, per_device(): jnp.dot(select, jnp.concatenate(lanes_in, axis=0), preferred_element_type...  4.41 us
    concatenate x1, other arithmetic, per_device(): jnp.concatenate([local_part, head_next], axis=0)  4.02 us
  transfers between devices with their start and end apart: 17, of which 10 were waited for; matrix products, arithmetic and copies ran while one was open for 10% of the time, Pallas kernels for 22%

profile of v1, /device:TPU:0, one launch (start us, length us, event | category | flops | bytes accessed | tf_op | source)
XLA Modules:
  0.0 178.7 jit_solution(5428188899554128362)
XLA Ops:
  6.6 1.0 copy-done
  7.5 1.2 fusion.6
  8.8 0.7 all-gather.12.cloned.1.call-update
  9.5 0.9 convert_reduce_fusion
  10.5 0.7 fusion.49
  18.6 1.9 %fusion.46 = (bf16[768,128]{1,0:T(8,128)(2,1)S(1)}, bf16[768,128]{1,0:T(8,128)(2,1)S(1)}, bf16[768,128]{1,0:T(8,128)(2,1)S(1)}, bf16[768,128]{1,0:T(8,128)(2,1)S(1)}) fusion(bf16[3072,512]{1,0:T(8,128)(2,1)} %param.9, s32[]{:T(128)S(6)} %select_n.227, s32[]{:T(128)S(6)} %select_n.228, s32[]{:T(128)S(6)} %select_n.229, s32[]{:T(128)S(6)} %select_n.231, ...), kind=kLoop, calls=%fused_computation.97 | loop fusion | bytes 1572884 | tf_op jit(solution)/shard_map/dynamic_slice | solution.py:235
  20.5 2.8 %collective-permute-start = (bf16[768,128]{1,0:T(8,128)(2,1)S(1)}, bf16[768,128]{1,0:T(8,128)(2,1)S(1)}, u32[]{:S(2)}, u32[]{:S(2)}) collective-permute-start(bf16[768,128]{1,0:T(8,128)(2,1)S(1)} %get-tuple-element.5), channel_id=1, source_target_pairs={{0,4},{4,8},{8,12},{12,16},{16,20},{20,24},{24,28},{28,0},{1,5},{5... | collective-permute-start | bytes 589832 | tf_op jit(solution)/shard_map/ppermute | solution.py:20
  23.3 3.1 %collective-permute-start.1 = (bf16[768,128]{1,0:T(8,128)(2,1)S(1)}, bf16[768,128]{1,0:T(8,128)(2,1)S(1)}, u32[]{:S(2)}, u32[]{:S(2)}) collective-permute-start(bf16[768,128]{1,0:T(8,128)(2,1)S(1)} %get-tuple-element.8), channel_id=1, source_target_pairs={{0,28},{4,0},{8,4},{12,8},{16,12},{20,16},{24,20},{28,24},{1,29},{... | collective-permute-start | bytes 589832 | tf_op jit(solution)/shard_map/ppermute | solution.py:20
  26.4 1.9 %collective-permute-start.2 = (bf16[768,128]{1,0:T(8,128)(2,1)S(1)}, bf16[768,128]{1,0:T(8,128)(2,1)S(1)}, u32[]{:S(2)}, u32[]{:S(2)}) collective-permute-start(bf16[768,128]{1,0:T(8,128)(2,1)S(1)} %get-tuple-element.7), channel_id=1, source_target_pairs={{0,24},{4,28},{8,0},{12,4},{16,8},{20,12},{24,16},{28,20},{1,25},{... | collective-permute-start | bytes 589832 | tf_op jit(solution)/shard_map/ppermute | solution.py:20
  28.3 0.1 select_reduce_fusion.1
  28.5 0.1 select_reduce_fusion
  28.6 3.5 %collective-permute-done = bf16[768,128]{1,0:T(8,128)(2,1)S(1)} collective-permute-done((bf16[768,128]{1,0:T(8,128)(2,1)S(1)}, bf16[768,128]{1,0:T(8,128)(2,1)S(1)}, u32[]{:S(2)}, u32[]{:S(2)}) %collective-permute-start) | collective-permute-done | bytes 196640 | tf_op jit(solution)/shard_map/ppermute | solution.py:20
  32.1 1.7 collective-permute-done.1
  33.8 1.0 collective-permute-done.2
  34.8 4.4 %fusion.5 = bf16[2048,128]{1,0:T(8,128)(2,1)S(1)} fusion(s32[2048]{0:T(1024)S(1)} %add_subtract_fusion, bf16[768,128]{1,0:T(8,128)(2,1)S(1)} %collective-permute-done.2, bf16[768,128]{1,0:T(8,128)(2,1)S(1)} %collective-permute-done.1, bf16[768,128]{1,0:T(8,128)(2,1)S(1)} %get-tuple-element.6, bf16[768,128]{1,0:T(8,128)(2,1)S(1)} %collective-permute-done), kind=kOutput, calls=%fused_computation.6 | convolution fusion | flops 1620312064 | bytes 1318912 | tf_op jit(solution)/shard_map/dot_general | solution.py:243
  39.3 2.4 %collective-permute-start.3 = (bf16[1024,128]{1,0:T(8,128)(2,1)S(1)}, bf16[1024,128]{1,0:T(8,128)(2,1)S(1)}, u32[]{:S(2)}, u32[]{:S(2)}) collective-permute-start(bf16[1024,128]{1,0:T(8,128)(2,1)S(1)} %slice.55), channel_id=1, source_target_pairs={{0,28},{4,0},{8,4},{12,8},{16,12},{20,16},{24,20},{28,24},{1,29},{... | collective-permute-start | bytes 786440 | tf_op jit(solution)/shard_map/ppermute | solution.py:20
  42.3 4.1 %collective-permute-done.3 = bf16[1024,128]{1,0:T(8,128)(2,1)S(1)} collective-permute-done((bf16[1024,128]{1,0:T(8,128)(2,1)S(1)}, bf16[1024,128]{1,0:T(8,128)(2,1)S(1)}, u32[]{:S(2)}, u32[]{:S(2)}) %collective-permute-start.3) | collective-permute-done | bytes 262176 | tf_op jit(solution)/shard_map/ppermute | solution.py:20
  46.5 4.0 %fusion.19 = (bf16[1024,128]{1,0:T(8,128)(2,1)S(1)}, bf16[1024,512]{1,0:T(8,128)(2,1)S(1)}, bf16[1024,128]{1,0:T(8,128)(2,1)S(1)}, bf16[1024,128]{1,0:T(8,128)(2,1)S(1)}) fusion(s32[]{:T(128)S(6)} %dynamic_slice.71, bf16[2048,128]{1,0:T(8,128)(2,1)S(1)} %fusion.5, bf16[1024,128]{1,0:T(8,128)(2,1)S(1)} %collective-permute-done.3, ...), kind=kLoop, calls=%fused_computation.30 | loop fusion | flops 2097152 | bytes 1835028 | tf_op jit(solution)/shard_map/concatenate | solution.py:248
  50.6 0.6 fusion.48
  51.2 1.4 collective-permute-start.5
  52.6 1.4 collective-permute-start.6
  54.0 17.1 %all-gather.1 = bf16[512,512]{1,0:T(8,128)(2,1)} all-gather(bf16[128,512]{1,0:T(8,128)(2,1)S(1)} %copy-done.3), channel_id=3, replica_groups=mesh['brick'=8,'mp'=4] {'mp'}, dimensions={0}, use_global_device_ids=true | all-gather | bytes 655360 | tf_op jit(solution)/shard_map/all_gather | solution.py:211
  71.4 2.9 %copy.11 = bf16[2048,384]{1,0:T(8,128)(2,1)} copy(bf16[2048,384]{0,1:T(8,128)(2,1)} %all-gather.8.cloned.1.call-done) | data formatting | bytes 3145728 | tf_op jit(solution)/shard_map/all_gather | solution.py:210
  74.3 38.7 %shard_map.91.attended = bf16[512,512]{1,0:T(8,128)(2,1)} custom-call(s32[1]{0:T(128)} %bitcast.query_from, bf16[1024,512]{1,0:T(8,128)(2,1)} %copy-done.2, f32[1,512]{1,0:T(1,128)} %get-tuple-element.23.gain, bf16[4,512,384]{2,1,0:T(8,128)(2,1)} %bitcast.18), custom_call_target="tpu_custom_call" | custom-call | flops 17179869184 | bytes 2097152 | tf_op jit(solution)/shard_map/pallas_call | solution.py:109
  113.1 7.0 %shard_map.92 = bf16[512,512]{1,0:T(8,128)(2,1)} custom-call(s32[1]{0:T(128)} %bitcast.query_from, bf16[1024,512]{1,0:T(8,128)(2,1)} %copy-done.2, bf16[512,512]{1,0:T(8,128)(2,1)} %shard_map.91.attended, f32[1,512]{1,0:T(1,128)} %get-tuple-element.22.gain, bf16[4,128,512]{2,1,0:T(8,128)(2,1)} %bitcast.19, bf16[4,512,512]{2,1,0:T(8,128)(2,1)} %bitcast.21, ...), custom_call_target="tpu_custom_call" | custom-call | flops 2147483648 | bytes 8388608 | tf_op jit(solution)/shard_map/pallas_call | solution.py:163
  120.2 1.2 constant_dynamic-slice_fusion
  121.4 0.4 collective-permute-start.7
  121.8 2.0 %collective-permute-start.8 = (bf16[512,128]{1,0:T(8,128)(2,1)S(1)}, bf16[512,128]{1,0:T(8,128)(2,1)S(1)}, u32[]{:S(2)}, u32[]{:S(2)}) collective-permute-start(bf16[512,128]{1,0:T(8,128)(2,1)S(1)} %get-tuple-element.17), channel_id=1, source_target_pairs={{0,2},{1,3},{2,0},{3,1},{4,6},{5,7},{6,4},{7,5},{8,10},{9,11},{10,... | collective-permute-start | bytes 393224 | tf_op jit(solution)/shard_map/ppermute | solution.py:20
  123.8 1.1 collective-permute-start.9
  124.9 1.9 %collective-permute-done.7 = bf16[512,128]{1,0:T(8,128)(2,1)S(1)} collective-permute-done((bf16[512,128]{1,0:T(8,128)(2,1)S(1)}, bf16[512,128]{1,0:T(8,128)(2,1)S(1)}, u32[]{:S(2)}, u32[]{:S(2)}) %collective-permute-start.7) | collective-permute-done | bytes 131104 | tf_op jit(solution)/shard_map/ppermute | solution.py:20
  126.8 1.3 collective-permute-done.8
  128.1 1.5 collective-permute-done.9
  129.7 3.4 %collective-permute-start.10 = (bf16[1024,128]{1,0:T(8,128)(2,1)S(1)}, bf16[1024,128]{1,0:T(8,128)(2,1)S(1)}, u32[]{:S(2)}, u32[]{:S(2)}) collective-permute-start(bf16[1024,128]{1,0:T(8,128)(2,1)S(1)} %slice.56), channel_id=1, source_target_pairs={{0,4},{4,8},{8,12},{12,16},{16,20},{20,24},{24,28},{28,0},{1,5},{5... | collective-permute-start | bytes 786440 | tf_op jit(solution)/shard_map/ppermute | solution.py:20
  133.1 9.6 %collective-permute-done.10 = bf16[1024,128]{1,0:T(8,128)(2,1)S(1)} collective-permute-done((bf16[1024,128]{1,0:T(8,128)(2,1)S(1)}, bf16[1024,128]{1,0:T(8,128)(2,1)S(1)}, u32[]{:S(2)}, u32[]{:S(2)}) %collective-permute-start.10) | collective-permute-done | bytes 262176 | tf_op jit(solution)/shard_map/ppermute | solution.py:20
  142.7 7.6 %fusion.4 = bf16[3072,128]{1,0:T(8,128)(2,1)S(1)} fusion(s32[2048]{0:T(1024)S(1)} %add_subtract_fusion, s32[]{:T(128)S(6)} %select_n.268, bf16[1024,128]{1,0:T(8,128)(2,1)S(1)} %collective-permute-done.10, bf16[2048,128]{1,0:T(8,128)(2,1)S(1)} %constant_dynamic-update-slice_fusion), kind=kOutput, calls=%fused_computation.5 | convolution fusion | flops 1618345984 | bytes 1581060 | tf_op jit(solution)/shard_map/dot_general | solution.py:289
  150.3 1.8 %collective-permute-start.11 = (bf16[768,128]{1,0:T(8,128)(2,1)S(1)}, bf16[768,128]{1,0:T(8,128)(2,1)S(1)}, u32[]{:S(2)}, u32[]{:S(2)}) collective-permute-start(bf16[768,128]{1,0:T(8,128)(2,1)S(1)} %slice.57), channel_id=1, source_target_pairs={{0,28},{4,0},{8,4},{12,8},{16,12},{20,16},{24,20},{28,24},{1,29},{... | collective-permute-start | bytes 589832 | tf_op jit(solution)/shard_map/ppermute | solution.py:20
  152.1 5.0 %collective-permute-done.11 = bf16[768,128]{1,0:T(8,128)(2,1)S(1)} collective-permute-done((bf16[768,128]{1,0:T(8,128)(2,1)S(1)}, bf16[768,128]{1,0:T(8,128)(2,1)S(1)}, u32[]{:S(2)}, u32[]{:S(2)}) %collective-permute-start.11) | collective-permute-done | bytes 196640 | tf_op jit(solution)/shard_map/ppermute | solution.py:20
  157.1 0.1 broadcast_in_dim.46
  157.2 0.6 dynamic_update_slice.44
  157.9 0.1 fusion.47
  158.0 0.6 dynamic_update_slice.45
  158.7 1.2 collective-permute-start.13
  159.9 8.7 %collective-permute-done.12 = bf16[768,128]{1,0:T(8,128)(2,1)S(1)} collective-permute-done((bf16[768,128]{1,0:T(8,128)(2,1)S(1)}, bf16[768,128]{1,0:T(8,128)(2,1)S(1)}, u32[]{:S(2)}, u32[]{:S(2)}) %collective-permute-start.12) | collective-permute-done | bytes 196640 | tf_op jit(solution)/shard_map/ppermute | solution.py:20
  168.5 0.1 dynamic-slice_add_fusion.1
  168.6 0.9 dynamic_update_slice.46
  169.6 0.1 dynamic-slice_add_fusion
  169.7 0.8 copy-done.1
  170.4 1.8 dynamic_update_slice.47
  (41 shorter events, 0.8 us)
Async XLA Ops:
  6.5 1.0 copy-start
  6.5 21.8 %copy-start.4 = (s32[2048]{0:T(1024)S(1)}, s32[2048]{0:T(1024)}, u32[]{:S(2)}) copy-start(s32[2048]{0:T(1024)} %param.11) | copy-start | bytes 24580
  6.5 64.8 %all-gather.8.cloned.1.call-start = ((), (), s32[]{:S(2)}) async-start(), calls=%async_computation | async-start | bytes 1966080 | tf_op jit(solution)/shard_map/all_gather | solution.py:210
  8.7 104.3 %all-gather.12.cloned.1.call-start = ((), (), s32[]{:S(2)}) async-start(), calls=%async_computation.2 | async-start | bytes 2621440 | tf_op jit(solution)/shard_map/all_gather | solution.py:213
  9.5 103.6 %all-gather.10.cloned.1.call-start = ((), (), s32[]{:S(2)}) async-start(), calls=%async_computation.1 | async-start | bytes 2621440 | tf_op jit(solution)/shard_map/all_gather | solution.py:212
  20.5 11.6 %collective-permute-start = (bf16[768,128]{1,0:T(8,128)(2,1)S(1)}, bf16[768,128]{1,0:T(8,128)(2,1)S(1)}, u32[]{:S(2)}, u32[]{:S(2)}) collective-permute-start(bf16[768,128]{1,0:T(8,128)(2,1)S(1)} %get-tuple-element.5), channel_id=1, source_target_pairs={{0,4},{4,8},{8,12},{12,16},{16,20},{20,24},{24,28},{28,0},{1,5},{5... | collective-permute-start | bytes 589832 | tf_op jit(solution)/shard_map/ppermute | solution.py:20
  23.3 10.6 %collective-permute-start.1 = (bf16[768,128]{1,0:T(8,128)(2,1)S(1)}, bf16[768,128]{1,0:T(8,128)(2,1)S(1)}, u32[]{:S(2)}, u32[]{:S(2)}) collective-permute-start(bf16[768,128]{1,0:T(8,128)(2,1)S(1)} %get-tuple-element.8), channel_id=1, source_target_pairs={{0,28},{4,0},{8,4},{12,8},{16,12},{20,16},{24,20},{28,24},{1,29},{... | collective-permute-start | bytes 589832 | tf_op jit(solution)/shard_map/ppermute | solution.py:20
  26.4 8.5 %collective-permute-start.2 = (bf16[768,128]{1,0:T(8,128)(2,1)S(1)}, bf16[768,128]{1,0:T(8,128)(2,1)S(1)}, u32[]{:S(2)}, u32[]{:S(2)}) collective-permute-start(bf16[768,128]{1,0:T(8,128)(2,1)S(1)} %get-tuple-element.7), channel_id=1, source_target_pairs={{0,24},{4,28},{8,0},{12,4},{16,8},{20,12},{24,16},{28,20},{1,25},{... | collective-permute-start | bytes 589832 | tf_op jit(solution)/shard_map/ppermute | solution.py:20
  39.2 11.3 %copy-start.5 = (f32[2,512]{1,0:T(2,128)S(1)}, f32[2,512]{1,0:T(2,128)}, u32[]{:S(2)}) copy-start(f32[2,512]{1,0:T(2,128)} %param.17) | copy-start | bytes 12292
  39.3 14.8 %copy-start.3 = (bf16[128,512]{1,0:T(8,128)(2,1)S(1)}, bf16[128,512]{1,0:T(8,128)(2,1)}, u32[]{:S(2)}) copy-start(bf16[128,512]{1,0:T(8,128)(2,1)} %param.14) | copy-start | bytes 393220
  39.3 7.1 %collective-permute-start.3 = (bf16[1024,128]{1,0:T(8,128)(2,1)S(1)}, bf16[1024,128]{1,0:T(8,128)(2,1)S(1)}, u32[]{:S(2)}, u32[]{:S(2)}) collective-permute-start(bf16[1024,128]{1,0:T(8,128)(2,1)S(1)} %slice.55), channel_id=1, source_target_pairs={{0,28},{4,0},{8,4},{12,8},{16,12},{20,16},{24,20},{28,24},{1,29},{... | collective-permute-start | bytes 786440 | tf_op jit(solution)/shard_map/ppermute | solution.py:20
  50.5 20.6 %collective-permute-start.4 = (bf16[1024,128]{1,0:T(8,128)(2,1)S(1)}, bf16[1024,128]{1,0:T(8,128)(2,1)S(1)}, u32[]{:S(2)}, u32[]{:S(2)}) collective-permute-start(bf16[1024,128]{1,0:T(8,128)(2,1)S(1)} %get-tuple-element.14), channel_id=1, source_target_pairs={{0,1},{1,2},{2,3},{3,0},{4,5},{5,6},{6,7},{7,4},{8,9},{9,10},{10,1... | collective-permute-start | bytes 786440 | tf_op jit(solution)/shard_map/ppermute | solution.py:20
  51.2 20.0 %collective-permute-start.5 = (bf16[1024,128]{1,0:T(8,128)(2,1)S(1)}, bf16[1024,128]{1,0:T(8,128)(2,1)S(1)}, u32[]{:S(2)}, u32[]{:S(2)}) collective-permute-start(bf16[1024,128]{1,0:T(8,128)(2,1)S(1)} %get-tuple-element.15), channel_id=1, source_target_pairs={{0,2},{1,3},{2,0},{3,1},{4,6},{5,7},{6,4},{7,5},{8,10},{9,11},{10,... | collective-permute-start | bytes 786440 | tf_op jit(solution)/shard_map/ppermute | solution.py:20
  52.6 18.7 %collective-permute-start.6 = (bf16[1024,128]{1,0:T(8,128)(2,1)S(1)}, bf16[1024,128]{1,0:T(8,128)(2,1)S(1)}, u32[]{:S(2)}, u32[]{:S(2)}) collective-permute-start(bf16[1024,128]{1,0:T(8,128)(2,1)S(1)} %get-tuple-element.12), channel_id=1, source_target_pairs={{0,3},{1,0},{2,1},{3,2},{4,7},{5,4},{6,5},{7,6},{8,11},{9,8},{10,9... | collective-permute-start | bytes 786440 | tf_op jit(solution)/shard_map/ppermute | solution.py:20
  71.3 3.0 %copy-start.2 = (bf16[1024,512]{1,0:T(8,128)(2,1)}, bf16[1024,512]{1,0:T(8,128)(2,1)S(1)}, u32[]{:S(2)}) copy-start(bf16[1024,512]{1,0:T(8,128)(2,1)S(1)} %constant_dynamic-update-slice_fusion.3.patch_rows) | copy-start | bytes 3145732
  121.4 5.4 %collective-permute-start.7 = (bf16[512,128]{1,0:T(8,128)(2,1)S(1)}, bf16[512,128]{1,0:T(8,128)(2,1)S(1)}, u32[]{:S(2)}, u32[]{:S(2)}) collective-permute-start(bf16[512,128]{1,0:T(8,128)(2,1)S(1)} %get-tuple-element.18), channel_id=1, source_target_pairs={{0,1},{1,2},{2,3},{3,0},{4,5},{5,6},{6,7},{7,4},{8,9},{9,10},{10,1... | collective-permute-start | bytes 393224 | tf_op jit(solution)/shard_map/ppermute | solution.py:20
  121.8 6.3 %collective-permute-start.8 = (bf16[512,128]{1,0:T(8,128)(2,1)S(1)}, bf16[512,128]{1,0:T(8,128)(2,1)S(1)}, u32[]{:S(2)}, u32[]{:S(2)}) collective-permute-start(bf16[512,128]{1,0:T(8,128)(2,1)S(1)} %get-tuple-element.17), channel_id=1, source_target_pairs={{0,2},{1,3},{2,0},{3,1},{4,6},{5,7},{6,4},{7,5},{8,10},{9,11},{10,... | collective-permute-start | bytes 393224 | tf_op jit(solution)/shard_map/ppermute | solution.py:20
  123.8 5.8 %collective-permute-start.9 = (bf16[512,128]{1,0:T(8,128)(2,1)S(1)}, bf16[512,128]{1,0:T(8,128)(2,1)S(1)}, u32[]{:S(2)}, u32[]{:S(2)}) collective-permute-start(bf16[512,128]{1,0:T(8,128)(2,1)S(1)} %get-tuple-element.16), channel_id=1, source_target_pairs={{0,3},{1,0},{2,1},{3,2},{4,7},{5,4},{6,5},{7,6},{8,11},{9,8},{10,9... | collective-permute-start | bytes 393224 | tf_op jit(solution)/shard_map/ppermute | solution.py:20
  129.7 13.0 %collective-permute-start.10 = (bf16[1024,128]{1,0:T(8,128)(2,1)S(1)}, bf16[1024,128]{1,0:T(8,128)(2,1)S(1)}, u32[]{:S(2)}, u32[]{:S(2)}) collective-permute-start(bf16[1024,128]{1,0:T(8,128)(2,1)S(1)} %slice.56), channel_id=1, source_target_pairs={{0,4},{4,8},{8,12},{12,16},{16,20},{20,24},{24,28},{28,0},{1,5},{5... | collective-permute-start | bytes 786440 | tf_op jit(solution)/shard_map/ppermute | solution.py:20
  150.3 6.8 %collective-permute-start.11 = (bf16[768,128]{1,0:T(8,128)(2,1)S(1)}, bf16[768,128]{1,0:T(8,128)(2,1)S(1)}, u32[]{:S(2)}, u32[]{:S(2)}) collective-permute-start(bf16[768,128]{1,0:T(8,128)(2,1)S(1)} %slice.57), channel_id=1, source_target_pairs={{0,28},{4,0},{8,4},{12,8},{16,12},{20,16},{24,20},{28,24},{1,29},{... | collective-permute-start | bytes 589832 | tf_op jit(solution)/shard_map/ppermute | solution.py:20
  158.0 10.6 %collective-permute-start.12 = (bf16[768,128]{1,0:T(8,128)(2,1)S(1)}, bf16[768,128]{1,0:T(8,128)(2,1)S(1)}, u32[]{:S(2)}, u32[]{:S(2)}) collective-permute-start(bf16[768,128]{1,0:T(8,128)(2,1)S(1)} %get-tuple-element.10), channel_id=1, source_target_pairs={{0,4},{4,8},{8,12},{12,16},{16,20},{20,24},{24,28},{28,0},{1,5},{5... | collective-permute-start | bytes 589832 | tf_op jit(solution)/shard_map/ppermute | solution.py:20
  158.7 10.9 %collective-permute-start.13 = (bf16[768,128]{1,0:T(8,128)(2,1)S(1)}, bf16[768,128]{1,0:T(8,128)(2,1)S(1)}, u32[]{:S(2)}, u32[]{:S(2)}) collective-permute-start(bf16[768,128]{1,0:T(8,128)(2,1)S(1)} %get-tuple-element.9), channel_id=1, source_target_pairs={{0,8},{4,12},{8,16},{12,20},{16,24},{20,28},{24,0},{28,4},{1,9},{5... | collective-permute-start | bytes 589832 | tf_op jit(solution)/shard_map/ppermute | solution.py:20
  169.6 0.9 copy-start.1
Sparse Core Ops, SparseCore 0:
  8.9 22.3 all-gather.7
  32.9 22.8 all-gather.11
  57.4 23.3 all-gather.9

commit v2 on v1

v2 whole, which is shorter than its diff:
```python
import functools
import math

import jax
import jax.numpy as jnp
from jax import lax
from jax.experimental import pallas as pl
from jax.experimental.pallas import tpu as pltpu
from jax.sharding import PartitionSpec as P

HEADS = 32
PATCH = 1024
EPSILON = 1e-05
VMEM_BYTES = 56 * 1024 * 1024


MESH = pl.DeviceIdType.MESH


def wrapped(value, count):
    value = jnp.where(value < 0, value + count, value)
    return jnp.where(value >= count, value - count, value)


def greet_all(bricks, parts):
    brick, part = lax.axis_index("brick"), lax.axis_index("mp")
    barrier = pltpu.get_barrier_semaphore()
    peers = [(0, step) for step in range(1, parts)]
    peers += [(away, step) for away in (-1, 1) for step in range(parts)]
    peers += [(-2, 0), (2, 0)]
    for away, step in peers:
        pl.semaphore_signal(
            barrier,
            inc=1,
            device_id=(lax.rem(brick + away + bricks, bricks), lax.rem(part + step, parts)),
            device_id_type=MESH,
        )
    pl.semaphore_wait(barrier, len(peers))


def enter_kernel(
    bricks,
    parts,
    index,
    slabs,
    patch_rows,
    arrived,
    total,
    merged,
    window_in,
    head_in,
    lane_send,
    lane_recv,
    window_send,
    window_recv,
    head_send,
    head_recv,
):
    brick, part = lax.axis_index("brick"), lax.axis_index("mp")
    slab_rows, width = slabs.shape[1], slabs.shape[2]
    rows = index.shape[0]
    tile = 512
    quarter = (rows - PATCH) // parts
    greet_all(bricks, parts)

    def lane_copy(lane):
        return pltpu.make_async_remote_copy(
            src_ref=slabs.at[lane],
            dst_ref=arrived.at[lane],
            send_sem=lane_send.at[lane],
            recv_sem=lane_recv.at[lane],
            device_id=(lax.rem(brick - lane + 1 + bricks, bricks), part),
            device_id_type=MESH,
        )

    for lane in (3, 0, 2):
        lane_copy(lane).start()

    def merge(lane, source, first):
        def one_tile(step, carry):
            at = pl.ds(pl.multiple_of(step * tile, tile), tile)
            spots = lax.broadcasted_iota(jnp.int32, (tile, slab_rows), 1) + lane * slab_rows
            chosen = (index[at, :] == spots).astype(jnp.bfloat16)
            term = jnp.dot(chosen, source, preferred_element_type=jnp.float32)
            if first:
                total[at, :] = term
            else:
                total[at, :] += term
            return carry

        lax.fori_loop(0, rows // tile, one_tile, 0)

    merge(1, slabs[1], True)
    for lane in (2, 0, 3):
        lane_copy(lane).wait()
        merge(lane, arrived[lane], False)
    merged[...] = total[...].astype(jnp.bfloat16)

    def patch_start(target):
        return pl.multiple_of((target * quarter // PATCH + 1) * PATCH, PATCH)

    last = rows - PATCH

    def head_copy(step):
        target = lax.rem(part + step, parts)
        return pltpu.make_async_remote_copy(
            src_ref=merged.at[pl.ds(0, PATCH)],
            dst_ref=head_in.at[step],
            send_sem=head_send.at[step],
            recv_sem=head_recv.at[step],
            device_id=(lax.rem(brick - 1 + bricks, bricks), target),
            device_id_type=MESH,
        )

    def window_copy(step):
        target = lax.rem(part + step, parts)
        return pltpu.make_async_remote_copy(
            src_ref=merged.at[pl.ds(patch_start(target), PATCH)],
            dst_ref=window_in.at[step],
            send_sem=window_send.at[step],
            recv_sem=window_recv.at[step],
            device_id=(brick, target),
            device_id_type=MESH,
        )

    for step in range(parts):

        @pl.when(patch_start(lax.rem(part + step, parts)) == last)
        def _():
            head_copy(step).start()

    for step in range(1, parts):
        window_copy(step).start()

    def columns(step):
        source = lax.rem(part - step + parts, parts)
        return pl.ds(pl.multiple_of(source * width, width), width)

    patch_rows[:, columns(0)] = merged[pl.ds(patch_start(part), PATCH), :]
    for step in range(1, parts):
        window_copy(step).wait()
        patch_rows[:, columns(step)] = window_in[step]

    @pl.when(patch_start(part) == last)
    def _():
        for step in range(parts):
            head_copy(step).wait_recv()
            patch_rows[:, columns(step)] += head_in[step]

    for step in range(parts):

        @pl.when(patch_start(lax.rem(part + step, parts)) == last)
        def _():
            head_copy(step).wait_send()


def enter(index, slabs, bricks, parts):
    lanes, slab_rows, width = slabs.shape
    rows = index.shape[0]
    whole = pl.BlockSpec(memory_space=pltpu.VMEM)
    return pl.pallas_call(
        functools.partial(enter_kernel, bricks, parts),
        out_shape=jax.ShapeDtypeStruct((PATCH, width * parts), jnp.bfloat16),
        in_specs=[whole, whole],
        out_specs=whole,
        scratch_shapes=[
            pltpu.VMEM((lanes, slab_rows, width), jnp.bfloat16),
            pltpu.VMEM((rows, width), jnp.float32),
            pltpu.VMEM((rows, width), jnp.bfloat16),
            pltpu.VMEM((parts, PATCH, width), jnp.bfloat16),
            pltpu.VMEM((parts, PATCH, width), jnp.bfloat16),
            pltpu.SemaphoreType.DMA((lanes,)),
            pltpu.SemaphoreType.DMA((lanes,)),
            pltpu.SemaphoreType.DMA((parts,)),
            pltpu.SemaphoreType.DMA((parts,)),
            pltpu.SemaphoreType.DMA((parts,)),
            pltpu.SemaphoreType.DMA((parts,)),
        ],
        compiler_params=pltpu.CompilerParams(
            collective_id=0, has_side_effects=True, vmem_limit_bytes=VMEM_BYTES
        ),
        cost_estimate=pl.CostEstimate(
            flops=2 * rows * lanes * slab_rows * width,
            bytes_accessed=20 * slab_rows * width * lanes,
            transcendentals=0,
        ),
    )(index, slabs)


def leave_kernel(
    bricks,
    parts,
    index,
    place,
    result,
    out,
    rows_in,
    leaving,
    arrived,
    total,
    window_send,
    window_recv,
    tail_send,
    tail_recv,
    lane_send,
    lane_recv,
):
    brick, part = lax.axis_index("brick"), lax.axis_index("mp")
    lanes, slab_rows, width = leaving.shape
    quarter = result.shape[1]
    capacity = out.shape[0]
    rows = rows_in.shape[0]
    tile = 512
    last = rows - PATCH
    greet_all(bricks, parts)

    def row_start(source):
        return PATCH + source * quarter

    def tail_copy(step):
        target = lax.rem(part + step, parts)
        start = pl.multiple_of(jnp.maximum(row_start(part) - last, 0), quarter)
        return pltpu.make_async_remote_copy(
            src_ref=result.at[target],
            dst_ref=rows_in.at[pl.ds(start, quarter)],
            send_sem=tail_send.at[step],
            recv_sem=tail_recv.at[part],
            device_id=(lax.rem(brick + 1, bricks), target),
            device_id_type=MESH,
        )

    def window_copy(step):
        target = lax.rem(part + step, parts)
        start = pl.multiple_of(row_start(part), quarter)
        return pltpu.make_async_remote_copy(
            src_ref=result.at[target],
            dst_ref=rows_in.at[pl.ds(start, quarter)],
            send_sem=window_send.at[step],
            recv_sem=window_recv.at[step],
            device_id=(brick, target),
            device_id_type=MESH,
        )

    def tail_arrival(source):
        return pltpu.make_async_remote_copy(
            src_ref=result.at[0],
            dst_ref=rows_in.at[pl.ds(row_start(source) - last, quarter)],
            send_sem=tail_send.at[0],
            recv_sem=tail_recv.at[source],
            device_id=(lax.rem(brick + 1, bricks), part),
            device_id_type=MESH,
        )

    def window_arrival(step):
        source = lax.rem(part - step + parts, parts)
        return pltpu.make_async_remote_copy(
            src_ref=result.at[0],
            dst_ref=rows_in.at[pl.ds(pl.multiple_of(row_start(source), quarter), quarter)],
            send_sem=window_send.at[step],
            recv_sem=window_recv.at[step],
            device_id=(brick, source),
            device_id_type=MESH,
        )

    sends_tail = row_start(part) >= last

    @pl.when(sends_tail)
    def _():
        for step in range(parts):
            tail_copy(step).start()

    for step in range(1, parts):
        window_copy(step).start()
    rows_in[pl.ds(pl.multiple_of(row_start(part), quarter), quarter), :] = result[part]
    for step in range(1, parts):
        window_arrival(step).wait_recv()
    for source in range(parts):
        if row_start(source) >= last:
            tail_arrival(source).wait_recv()

    def lane_copy(lane):
        return pltpu.make_async_remote_copy(
            src_ref=leaving.at[lane],
            dst_ref=arrived.at[lane],
            send_sem=lane_send.at[lane],
            recv_sem=lane_recv.at[lane],
            device_id=(lax.rem(brick + lane - 1 + bricks, bricks), part),
            device_id_type=MESH,
        )

    third = slab_rows // 3

    def spread(lane):
        def one_tile(step, carry):
            start = pl.multiple_of(step * third, third)
            spots = (
                lax.broadcasted_iota(jnp.int32, (third, rows), 0) + lane * slab_rows + start
            )
            chosen = (index[...] == spots).astype(jnp.bfloat16)
            leaving[lane, pl.ds(start, third), :] = jnp.dot(
                chosen, rows_in[...], preferred_element_type=jnp.float32
            ).astype(jnp.bfloat16)
            return carry

        lax.fori_loop(0, 3, one_tile, 0)

    for lane in (3, 0, 2):
        spread(lane)
        lane_copy(lane).start()
    spread(1)

    def put(lane, source, first, final):
        def one_tile(step, carry):
            at = pl.ds(pl.multiple_of(step * tile, tile), tile)
            spots = lax.broadcasted_iota(jnp.int32, (tile, slab_rows), 1) + lane * slab_rows
            chosen = (place[at, :] == spots).astype(jnp.bfloat16)
            term = jnp.dot(chosen, source, preferred_element_type=jnp.float32)
            if not first:
                term = total[at, :] + term
            if final:
                out[at, :] = term.astype(jnp.bfloat16)
            else:
                total[at, :] = term
            return carry

        lax.fori_loop(0, capacity // tile, one_tile, 0)

    put(1, leaving[1], True, False)
    for lane in (2, 0, 3):
        lane_copy(lane).wait()
        put(lane, arrived[lane], False, lane == 3)

    for step in range(1, parts):
        window_copy(step).wait_send()

    @pl.when(sends_tail)
    def _():
        for step in range(parts):
            tail_copy(step).wait_send()


def leave(index, place, result, bricks, lanes, slab_rows):
    parts, quarter, width = result.shape
    rows = index.shape[1]
    capacity = place.shape[0]
    whole = pl.BlockSpec(memory_space=pltpu.VMEM)
    return pl.pallas_call(
        functools.partial(leave_kernel, bricks, parts),
        out_shape=jax.ShapeDtypeStruct((capacity, width), jnp.bfloat16),
        in_specs=[whole, whole, whole],
        out_specs=whole,
        scratch_shapes=[
            pltpu.VMEM((rows, width), jnp.bfloat16),
            pltpu.VMEM((lanes, slab_rows, width), jnp.bfloat16),
            pltpu.VMEM((lanes, slab_rows, width), jnp.bfloat16),
            pltpu.VMEM((capacity, width), jnp.float32),
            pltpu.SemaphoreType.DMA((parts,)),
            pltpu.SemaphoreType.DMA((parts,)),
            pltpu.SemaphoreType.DMA((parts,)),
            pltpu.SemaphoreType.DMA((parts,)),
            pltpu.SemaphoreType.DMA((lanes,)),
            pltpu.SemaphoreType.DMA((lanes,)),
        ],
        compiler_params=pltpu.CompilerParams(
            collective_id=1, has_side_effects=True, vmem_limit_bytes=VMEM_BYTES
        ),
        cost_estimate=pl.CostEstimate(
            flops=4 * rows * lanes * slab_rows * width,
            bytes_accessed=20 * slab_rows * width * lanes,
            transcendentals=0,
        ),
    )(index, place, result)


def layer_norm(values, gain):
    centred = values - jnp.mean(values, axis=-1, keepdims=True)
    spread = jnp.mean(centred * centred, axis=-1, keepdims=True)
    return (centred * lax.rsqrt(spread + EPSILON) * gain).astype(jnp.bfloat16)


def attention_kernel(
    head_dim,
    query_tile,
    query_from,
    patch_rows,
    gain,
    weights,
    attended,
    normed,
    queries,
    keys,
    values,
):
    groups, _, triple = weights.shape
    lanes = triple // 3
    group_heads = lanes // head_dim
    query_rows = attended.shape[0]
    normed[...] = layer_norm(patch_rows[...].astype(jnp.float32), gain[...])
    start = pl.multiple_of(query_from[0], query_rows)
    scale = head_dim ** (-0.5) * math.log2(math.e)
    lane_head = lax.broadcasted_iota(jnp.int32, (1, lanes), 1) // head_dim
    for group in range(groups):
        weight = weights[group]
        queries[group] = (
            jnp.dot(
                normed[pl.ds(start, query_rows), :],
                weight[:, :lanes],
                preferred_element_type=jnp.float32,
            )
            * scale
        ).astype(jnp.bfloat16)
        both = jnp.dot(
            normed[...], weight[:, lanes:], preferred_element_type=jnp.float32
        ).astype(jnp.bfloat16)
        keys[group] = both[:, :lanes]
        values[group, :, :lanes] = both[:, lanes:]
        values[group, :, lanes:] = jnp.ones_like(both[:, lanes:])

    def one_group(group, carry):
        attended_group = [
            jnp.zeros((query_tile, lanes), jnp.float32)
            for _ in range(query_rows // query_tile)
        ]

        def one_head(head, sums):
            mine = lane_head == head
            results = []
            for tile in range(query_rows // query_tile):
                query = queries[group, tile * query_tile : (tile + 1) * query_tile, :]
                query = jnp.where(mine, query, jnp.zeros_like(query))
                scores = lax.dot_general(
                    query,
                    keys[group],
                    (((1,), (1,)), ((), ())),
                    preferred_element_type=jnp.float32,
                )
                highest = jnp.max(scores, axis=-1, keepdims=True)
                exps = jnp.exp2((scores - highest).astype(jnp.bfloat16))
                product = jnp.dot(
                    exps, values[group], preferred_element_type=jnp.float32
                )
                result = product[:, :lanes] / product[:, lanes:]
                results.append(jnp.where(mine, result, sums[tile]))
            return tuple(results)

        sums = lax.fori_loop(0, group_heads, one_head, tuple(attended_group), unroll=2)
        for tile in range(query_rows // query_tile):
            attended[tile * query_tile : (tile + 1) * query_tile, pl.ds(
                pl.multiple_of(group * lanes, lanes), lanes
            )] = sums[tile].astype(jnp.bfloat16)
        return carry

    lax.fori_loop(0, groups, one_group, 0)


def attention(patch_rows, gain, weights, query_from, query_rows, head_dim):
    groups, width, triple = weights.shape
    lanes = triple // 3
    rows = patch_rows.shape[0]
    whole = pl.BlockSpec(memory_space=pltpu.VMEM)
    return pl.pallas_call(
        functools.partial(attention_kernel, head_dim, query_rows),
        out_shape=jax.ShapeDtypeStruct((query_rows, groups * lanes), jnp.bfloat16),
        in_specs=[pl.BlockSpec(memory_space=pltpu.SMEM), whole, whole, whole],
        out_specs=whole,
        scratch_shapes=[
            pltpu.VMEM((rows, width), jnp.bfloat16),
            pltpu.VMEM((groups, query_rows, lanes), jnp.bfloat16),
            pltpu.VMEM((groups, rows, lanes), jnp.bfloat16),
            pltpu.VMEM((groups, rows, 2 * lanes), jnp.bfloat16),
        ],
        compiler_params=pltpu.CompilerParams(vmem_limit_bytes=VMEM_BYTES),
        cost_estimate=pl.CostEstimate(
            flops=4 * rows * query_rows * groups * lanes * 16,
            bytes_accessed=4 * rows * width,
            transcendentals=rows * query_rows * groups * 8,
        ),
    )(query_from, patch_rows, gain, weights)


def mlp_kernel(query_from, patch_rows, attended, gain, weights, result):
    groups, _, width_full = weights.shape
    rows = attended.shape[0]
    depth = attended.shape[1] // groups
    hidden_part = (weights.shape[1] - depth) // 2
    proj_weight = [weights[group, :depth, :] for group in range(groups)]
    up_weight = [weights[group, depth : depth + hidden_part, :] for group in range(groups)]
    down_weight = [weights[group, depth + hidden_part :, :] for group in range(groups)]
    start = pl.multiple_of(query_from[0], rows)
    own = patch_rows[pl.ds(start, rows), :].astype(jnp.float32)
    mixed = None
    for group in range(groups):
        term = jnp.dot(
            attended[:, group * depth : (group + 1) * depth],
            proj_weight[group],
            preferred_element_type=jnp.float32,
        ).astype(jnp.bfloat16).astype(jnp.float32)
        mixed = term if mixed is None else mixed + term
    hidden = (own + mixed).astype(jnp.bfloat16).astype(jnp.float32)
    normed = layer_norm(hidden, gain[...])
    total = None
    for group in range(groups):
        expanded = jnp.dot(normed, up_weight[group], preferred_element_type=jnp.float32)
        expanded = (
            0.5 * expanded * (1.0 + lax.erf(expanded * math.sqrt(0.5)))
        ).astype(jnp.bfloat16)
        term = jnp.dot(
            expanded, down_weight[group], preferred_element_type=jnp.float32
        ).astype(jnp.bfloat16).astype(jnp.float32)
        total = term if total is None else total + term
    final = (hidden + total).astype(jnp.bfloat16)
    width = result.shape[2]
    for part in range(result.shape[0]):
        result[part] = final[:, part * width : (part + 1) * width]


def mlp(patch_rows, attended, gain, weights, query_from):
    whole = pl.BlockSpec(memory_space=pltpu.VMEM)
    rows, width = attended.shape
    groups, hidden = weights.shape[0], weights.shape[2]
    return pl.pallas_call(
        mlp_kernel,
        out_shape=jax.ShapeDtypeStruct((groups, rows, width // groups), jnp.bfloat16),
        in_specs=[pl.BlockSpec(memory_space=pltpu.SMEM)] + [whole] * 4,
        out_specs=whole,
        compiler_params=pltpu.CompilerParams(vmem_limit_bytes=VMEM_BYTES),
        cost_estimate=pl.CostEstimate(
            flops=4 * rows * width * hidden * groups,
            bytes_accessed=8 * width * hidden * groups,
            transcendentals=rows * hidden * groups,
        ),
    )(query_from, patch_rows, attended, gain, weights)


def per_device(
    voxel_feats,
    slot_rank,
    curve_order,
    patch_shift,
    qkv_weight,
    proj_weight,
    up_weight,
    down_weight,
    norm_gains,
):
    bricks = lax.axis_size("brick")
    model_parts = lax.axis_size("mp")
    my_index = lax.axis_index("brick")
    part_index = lax.axis_index("mp")
    capacity = voxel_feats.shape[0]
    shard_rows = curve_order.shape[0]
    pair_rows = 3 * (shard_rows // 8)
    width_full = voxel_feats.shape[1]
    width_part = width_full // model_parts
    quarter_rows = shard_rows // model_parts
    head_dim = width_full // HEADS
    offset = patch_shift[0].astype(jnp.uint32)
    latest = capacity - pair_rows

    triple = qkv_weight.shape[1]
    spot = jnp.arange(triple, dtype=jnp.int32)
    kind, within = spot // width_part, spot % width_part
    origin = (within // head_dim) * 3 * head_dim + kind * head_dim + within % head_dim
    shuffle = (spot[:, None] == origin[None, :]).astype(jnp.bfloat16)
    qkv_sorted = jnp.dot(
        qkv_weight, shuffle, preferred_element_type=jnp.float32
    ).astype(jnp.bfloat16)
    qkv_all = lax.all_gather(qkv_sorted, "mp", axis=0)
    mlp_all = lax.all_gather(
        jnp.concatenate([proj_weight, up_weight, down_weight], axis=0), "mp", axis=0
    )

    lane_ids = jnp.arange(4, dtype=jnp.int32)
    lane_targets = wrapped(my_index - (lane_ids - 1), bricks)
    low = lane_targets * shard_rows
    below = slot_rank[:, None] < low[None, :]
    upto = slot_rank[:, None] < (low + shard_rows)[None, :]
    run_starts = jnp.sum(below.astype(jnp.int32), axis=0)
    slab_starts = jnp.minimum(run_starts, latest)
    in_run = jnp.logical_and(upto, jnp.logical_not(below))
    slot_ids = jnp.arange(capacity, dtype=jnp.int32)
    spots = slot_ids[:, None] + (lane_ids * pair_rows - slab_starts)[None, :] + 1
    place = jnp.sum(jnp.where(in_run, spots, 0), axis=1, keepdims=True) - 1

    source_brick = curve_order // capacity
    source_slot = curve_order - source_brick * capacity
    source_lane = wrapped(source_brick - my_index + 1, bricks)
    from_lane = source_lane[:, None] == lane_ids[None, :]
    first_slot = jnp.min(jnp.where(from_lane, source_slot[:, None], latest), axis=0)
    first_of_row = jnp.sum(jnp.where(from_lane, first_slot[None, :], 0), axis=1)
    recv_index = source_lane * pair_rows + source_slot - first_of_row
    empty = jnp.full((PATCH,), -1, jnp.int32)
    index = lax.dynamic_slice_in_dim(
        jnp.concatenate([empty, recv_index, empty]), offset, shard_rows + PATCH, 0
    )

    column = (part_index * width_part).astype(jnp.uint32)
    starts = slab_starts.astype(jnp.uint32)
    slabs = jnp.stack(
        [
            lax.dynamic_slice(voxel_feats, (starts[lane], column), (pair_rows, width_part))
            for lane in range(4)
        ]
    )
    patch_rows = enter(index[:, None], slabs, bricks, model_parts)
    query_from = (lax.rem(part_index * quarter_rows, PATCH))[None]
    attended = attention(
        patch_rows, norm_gains[0:1], qkv_all, query_from, quarter_rows, head_dim
    )
    result = mlp(patch_rows, attended, norm_gains[1:2], mlp_all, query_from)
    return leave(index[None, :], place, result, bricks, 4, pair_rows)


def solution(mesh):
    return jax.shard_map(
        per_device,
        mesh=mesh,
        in_specs=(
            P("brick", None),
            P("brick"),
            P("brick"),
            P(),
            P(None, "mp"),
            P("mp", None),
            P(None, "mp"),
            P("mp", None),
            P(),
        ),
        out_specs=P("brick", "mp"),
        check_vma=False,
    )
```

time: 179 us -> 187 us (1.045)
  Pallas kernels: 45.8 us -> 152 us
  waiting for transfers between devices: 39 us -> 0.06 us
  starting transfers between devices: 23.2 us -> 0.04 us
  blocking collectives: 17.1 us -> 0 us
  matrix products: 13.2 us -> 1.17 us
  between operations: 21.5 us -> 14.2 us
    pallas_call x2 -> x4, Pallas kernels: 45.8 us -> 152 us  [the longest x1 59.6 us: enter(): pl.pallas_call(functools.partial(enter_kernel, bricks, parts), out_shape=...]
    ppermute x14 -> x0, waiting for transfers between devices: 38.2 us -> none  [shifted(): return lax.ppermute(value, axis, pairs)]
    ppermute x14 -> x0, starting transfers between devices: 23.1 us -> none  [shifted(): return lax.ppermute(value, axis, pairs)]
    all_gather x1 -> x0, blocking collectives: 17.1 us -> none  [per_device(): proj_all = lax.all_gather(proj_weight, 'mp', axis=0)]
    dot_general x2 -> x0, matrix products: 12 us -> none  [the longest x1 7.58 us: per_device(): lax.dot_general(select, own_rows, (((0,), (0,)), ((), ())), preferred_ele...]
    another operation x0 -> x1, local copies, waits for them, and re-layouts: none -> 4.51 us  [per_device(): jnp.stack([lax.dynamic_slice(voxel_feats, (starts[lane], column), (pair_r...]
    dynamic_update_slice x10 -> x0, local copies, waits for them, and re-layouts: 4.22 us -> none  [the longest x4 3.96 us: per_device(): lax.dynamic_update_slice_in_dim(out, before + piece, slab_starts[lane], 0)]
    dynamic_slice x2 -> x0, local copies, waits for them, and re-layouts: 3.02 us -> none  [the longest x1 1.85 us: per_device(): lax.dynamic_slice(voxel_feats, (slab_starts[lane], part_index * width_par...]
  transfers between devices with their start and end apart: 17 -> 2, of which waited for: 10 -> 0; matrix products, arithmetic and copies ran while one was open for 10% -> 8% of each run, Pallas kernels for 22% -> 52%
where the time goes in v2:
time: 187 us; the launch traced here: 186 us
  Pallas kernels  152 us (81%)
  local copies, waits for them, and re-layouts  14.9 us (8%)
  between operations  14.2 us (8%)
  other arithmetic  3.7 us (2%)
    pallas_call x1, Pallas kernels, enter(): pl.pallas_call(functools.partial(enter_kernel, bricks, parts), out_shape=...  59.6 us
    pallas_call x1, Pallas kernels, leave(): pl.pallas_call(functools.partial(leave_kernel, bricks, parts), out_shape=...  48.9 us
    pallas_call x1, Pallas kernels, attention(): pl.pallas_call(functools.partial(attention_kernel, head_dim, query_rows),...  36.1 us
    pallas_call x1, Pallas kernels, mlp(): pl.pallas_call(mlp_kernel, out_shape=jax.ShapeDtypeStruct((groups, rows,...  7.02 us
    another operation x1, local copies, waits for them, and re-layouts, per_device(): jnp.stack([lax.dynamic_slice(voxel_feats, (starts[lane], column), (pair_r...  4.51 us
  transfers between devices with their start and end apart: 2, of which 0 were waited for; matrix products, arithmetic and copies ran while one was open for 8% of the time, Pallas kernels for 52%

profile of v2, /device:TPU:0, one launch (start us, length us, event | category | flops | bytes accessed | tf_op | source)
XLA Modules:
  0.0 185.6 jit_solution(11131310600863241998)
XLA Ops:
  6.5 0.0 copy-start
  6.5 0.0 copy-start.2
  6.5 0.0 copy-start.1
  6.5 0.0 all-gather.5.cloned.1.call-start
  6.6 1.0 copy-done
  7.5 1.2 fusion
  8.7 0.0 all-gather.5.cloned.1.call-update
  8.7 0.0 copy-start.5
  8.7 0.0 all-gather.7.cloned.1.call-start
  8.8 0.0 copy-done.2
  8.8 0.0 copy-done.1
  8.8 2.0 %pad_maximum_fusion = bf16[1152,512]{1,0:T(8,128)(2,1)} fusion(bf16[512,512]{1,0:T(8,128)(2,1)S(1)} %copy-done.1, bf16[512,512]{1,0:T(8,128)(2,1)S(1)} %copy-done.2, bf16[128,512]{1,0:T(8,128)(2,1)} %param.14), kind=kLoop, calls=%fused_computation.2 | loop fusion | flops 3538944 | bytes 2359296 | tf_op jit(solution)/shard_map/concatenate | solution.py:570
  10.8 0.0 copy-start.4
  10.8 0.0 all-gather.7.cloned.1.call-update
  11.5 0.0 copy-done.5
  11.5 0.1 select_reduce_fusion.2
  11.6 0.1 select_reduce_fusion.1
  11.8 0.1 fusion.7
  11.9 0.0 copy-start.3
  11.9 1.7 copy.14.index
  13.6 0.0 copy-done.4
  13.6 0.2 fusion.4
  13.8 0.1 select_reduce_fusion
  14.0 1.7 copy.16.place
  15.7 0.0 copy-done.3
  15.7 0.7 fusion.24
  16.3 0.0 copy-start.6
  16.3 4.5 %dynamic-slice_bitcast_fusion.3 = (bf16[1,768,128]{2,1,0:T(8,128)(2,1)S(1)}, bf16[1,768,128]{2,1,0:T(8,128)(2,1)S(1)}, bf16[1,768,128]{2,1,0:T(8,128)(2,1)S(1)}, bf16[1,768,128]{2,1,0:T(8,128)(2,1)S(1)}) fusion(bf16[3072,512]{1,0:T(8,128)(2,1)} %param.9, u32[]{:T(128)} %bitcast.5, u32[]{:T(128)S(6)} %convert_element_type.26, u32[]{:T(128)} %bitcast.7, ...), kind=kLoop, calls=%fused_computation.10 | loop fusion | bytes 1572884 | tf_op jit(solution)/shard_map/stack | solution.py:599
  20.8 1.0 pad_maximum_fusion.1.slabs
  21.8 0.0 copy-done.6
  21.8 0.6 fusion.23
  22.4 59.6 %shard_map.91.patch_rows = bf16[1024,512]{1,0:T(8,128)(2,1)} custom-call(s32[3072,1]{1,0:T(8,128)} %copy.14.index, bf16[4,768,128]{2,1,0:T(8,128)(2,1)} %pad_maximum_fusion.1.slabs), custom_call_target="tpu_custom_call" | custom-call | flops 2415919104 | bytes 7864320 | tf_op jit(solution)/shard_map/pallas_call | solution.py:161
  82.0 0.0 all-gather.5.cloned.1.call-done
  82.0 2.7 %copy.15 = bf16[2048,384]{1,0:T(8,128)(2,1)} copy(bf16[2048,384]{0,1:T(8,128)(2,1)} %all-gather.5.cloned.1.call-done) | data formatting | bytes 3145728 | tf_op jit(solution)/shard_map/all_gather | solution.py:568
  84.7 36.1 %shard_map.92.attended = bf16[512,512]{1,0:T(8,128)(2,1)} custom-call(s32[1]{0:T(128)} %bitcast.3.query_from, bf16[1024,512]{1,0:T(8,128)(2,1)} %shard_map.91.patch_rows, f32[1,512]{1,0:T(1,128)} %get-tuple-element.12.gain, bf16[4,512,384]{2,1,0:T(8,128)(2,1)} %bitcast.22), custom_call_target="tpu_custom_call" | custom-call | flops 17179869184 | bytes 2097152 | tf_op jit(solution)/shard_map/pallas_call | solution.py:461
  120.8 0.0 all-gather.7.cloned.1.call-done
  120.8 7.0 %shard_map.93.result = bf16[4,512,128]{2,1,0:T(8,128)(2,1)} custom-call(s32[1]{0:T(128)} %bitcast.3.query_from, bf16[1024,512]{1,0:T(8,128)(2,1)} %shard_map.91.patch_rows, bf16[512,512]{1,0:T(8,128)(2,1)} %shard_map.92.attended, f32[1,512]{1,0:T(1,128)} %get-tuple-element.11.gain, bf16[4,1152,512]{2,1,0:T(8,128)(2,1)} %bitcast.26), custom_call_target="tpu_custom_call" | custom-call | flops 2147483648 | bytes 8388608 | tf_op jit(solution)/shard_map/pallas_call | solution.py:521
  127.8 48.9 %shard_map.94 = bf16[3072,128]{1,0:T(8,128)(2,1)} custom-call(s32[1,3072]{1,0:T(1,128)} %bitcast.24, s32[3072,1]{1,0:T(8,128)} %copy.16.place, bf16[4,512,128]{2,1,0:T(8,128)(2,1)} %shard_map.93.result), custom_call_target="tpu_custom_call" | custom-call | flops 4831838208 | bytes 7864320 | tf_op jit(solution)/shard_map/pallas_call | solution.py:347
  176.7 2.1 %copy.19 = bf16[3072,128]{1,0:T(8,128)(2,1)} copy(bf16[3072,128]{1,0:T(8,128)(2,1)} %shard_map.94) | data formatting | bytes 1572864
  (7 shorter events, 0.1 us)
Async XLA Ops:
  6.5 1.0 copy-start
  6.5 2.3 %copy-start.2 = (bf16[512,512]{1,0:T(8,128)(2,1)S(1)}, bf16[512,512]{1,0:T(8,128)(2,1)}, u32[]{:S(2)}) copy-start(bf16[512,512]{1,0:T(8,128)(2,1)} %param.15) | copy-start | bytes 1572868
  6.5 2.3 %copy-start.1 = (bf16[512,512]{1,0:T(8,128)(2,1)S(1)}, bf16[512,512]{1,0:T(8,128)(2,1)}, u32[]{:S(2)}) copy-start(bf16[512,512]{1,0:T(8,128)(2,1)} %param.16) | copy-start | bytes 1572868
  6.5 75.5 %all-gather.5.cloned.1.call-start = ((), (), s32[]{:S(2)}) async-start(), calls=%async_computation | async-start | bytes 1966080 | tf_op jit(solution)/shard_map/all_gather | solution.py:568
  8.7 2.8 %copy-start.5 = (s32[2048]{0:T(1024)S(1)}, s32[2048]{0:T(1024)}, u32[]{:S(2)}) copy-start(s32[2048]{0:T(1024)} %param.11) | copy-start | bytes 24580
  8.7 112.0 %all-gather.7.cloned.1.call-start = ((), (), s32[]{:S(2)}) async-start(), calls=%async_computation.1 | async-start | bytes 5898240 | tf_op jit(solution)/shard_map/all_gather | solution.py:569
  10.8 2.8 %copy-start.4 = (s32[3072]{0:T(1024)S(1)}, s32[3072]{0:T(1024)}, u32[]{:S(2)}) copy-start(s32[3072]{0:T(1024)} %param.10) | copy-start | bytes 36868
  11.9 3.8 %copy-start.3 = (s32[3072]{0:T(1024)}, s32[3072]{0:T(1024)S(1)}, u32[]{:S(2)}) copy-start(s32[3072]{0:T(1024)S(1)} %fusion.7) | copy-start | bytes 36868
  16.3 5.5 %copy-start.6 = (f32[2,512]{1,0:T(2,128)S(1)}, f32[2,512]{1,0:T(2,128)}, u32[]{:S(2)}) copy-start(f32[2,512]{1,0:T(2,128)} %param.17) | copy-start | bytes 12292
Sparse Core Ops, SparseCore 0:
  8.9 22.3 all-gather.4
  32.9 56.2 all-gather.6

commit v3 on v2

--- a/solution.py
+++ b/solution.py
@@ -11,10 +11,21 @@
 HEADS = 32
 PATCH = 1024
 EPSILON = 1e-05
+ALIGN = 16
 VMEM_BYTES = 56 * 1024 * 1024
 
 
 MESH = pl.DeviceIdType.MESH
+
+
+def gathered(value, reach):
+    parts = lax.axis_size("mp")
+    half = parts // 2
+    if reach == "far":
+        groups = [[first, first + half] for first in range(half)]
+    else:
+        groups = [list(range(half)), list(range(half, parts))]
+    return lax.all_gather(value, "mp", axis=0, tiled=True, axis_index_groups=groups)
 
 
 def wrapped(value, count):
@@ -49,6 +60,7 @@
     merged,
     window_in,
     head_in,
+    column_index,
     lane_send,
     lane_recv,
     window_send,
@@ -58,8 +70,9 @@
 ):
     brick, part = lax.axis_index("brick"), lax.axis_index("mp")
     slab_rows, width = slabs.shape[1], slabs.shape[2]
-    rows = index.shape[0]
-    tile = 512
+    rows = index.shape[1]
+    tile = 1024
+    lane_width = column_index.shape[1]
     quarter = (rows - PATCH) // parts
     greet_all(bricks, parts)
 
@@ -75,12 +88,23 @@
 
     for lane in (3, 0, 2):
         lane_copy(lane).start()
+    for start in range(0, rows, tile):
+        column_index[start : start + tile, :] = jnp.broadcast_to(
+            index[:, start : start + tile], (lane_width, tile)
+        ).T
 
     def merge(lane, source, first):
         def one_tile(step, carry):
             at = pl.ds(pl.multiple_of(step * tile, tile), tile)
-            spots = lax.broadcasted_iota(jnp.int32, (tile, slab_rows), 1) + lane * slab_rows
-            chosen = (index[at, :] == spots).astype(jnp.bfloat16)
+            mine = column_index[at, :] - lane * slab_rows
+            spots = lax.broadcasted_iota(jnp.int32, (tile, lane_width), 1)
+            chosen = jnp.concatenate(
+                [
+                    jnp.where(mine == spots + start, 1.0, 0.0).astype(jnp.bfloat16)
+                    for start in range(0, slab_rows, lane_width)
+                ],
+                axis=1,
+            )
             term = jnp.dot(chosen, source, preferred_element_type=jnp.float32)
             if first:
                 total[at, :] = term
@@ -156,7 +180,7 @@
 
 def enter(index, slabs, bricks, parts):
     lanes, slab_rows, width = slabs.shape
-    rows = index.shape[0]
+    rows = index.shape[1]
     whole = pl.BlockSpec(memory_space=pltpu.VMEM)
     return pl.pallas_call(
         functools.partial(enter_kernel, bricks, parts),
@@ -169,6 +193,7 @@
             pltpu.VMEM((rows, width), jnp.bfloat16),
             pltpu.VMEM((parts, PATCH, width), jnp.bfloat16),
             pltpu.VMEM((parts, PATCH, width), jnp.bfloat16),
+            pltpu.VMEM((rows, 128), jnp.int32),
             pltpu.SemaphoreType.DMA((lanes,)),
             pltpu.SemaphoreType.DMA((lanes,)),
             pltpu.SemaphoreType.DMA((parts,)),
@@ -191,13 +216,10 @@
     bricks,
     parts,
     index,
-    place,
     result,
-    out,
+    arrived,
     rows_in,
     leaving,
-    arrived,
-    total,
     window_send,
     window_recv,
     tail_send,
@@ -208,9 +230,7 @@
     brick, part = lax.axis_index("brick"), lax.axis_index("mp")
     lanes, slab_rows, width = leaving.shape
     quarter = result.shape[1]
-    capacity = out.shape[0]
     rows = rows_in.shape[0]
-    tile = 512
     last = rows - PATCH
     greet_all(bricks, parts)
 
@@ -288,47 +308,19 @@
             device_id_type=MESH,
         )
 
-    third = slab_rows // 3
-
     def spread(lane):
-        def one_tile(step, carry):
-            start = pl.multiple_of(step * third, third)
-            spots = (
-                lax.broadcasted_iota(jnp.int32, (third, rows), 0) + lane * slab_rows + start
-            )
-            chosen = (index[...] == spots).astype(jnp.bfloat16)
-            leaving[lane, pl.ds(start, third), :] = jnp.dot(
-                chosen, rows_in[...], preferred_element_type=jnp.float32
-            ).astype(jnp.bfloat16)
-            return carry
-
-        lax.fori_loop(0, 3, one_tile, 0)
+        spots = lax.broadcasted_iota(jnp.int32, (slab_rows, rows), 0) + lane * slab_rows
+        chosen = jnp.where(index[...] == spots, 1.0, 0.0).astype(jnp.bfloat16)
+        return jnp.dot(
+            chosen, rows_in[...], preferred_element_type=jnp.float32
+        ).astype(jnp.bfloat16)
 
     for lane in (3, 0, 2):
-        spread(lane)
+        leaving[lane] = spread(lane)
         lane_copy(lane).start()
-    spread(1)
-
-    def put(lane, source, first, final):
-        def one_tile(step, carry):
-            at = pl.ds(pl.multiple_of(step * tile, tile), tile)
-            spots = lax.broadcasted_iota(jnp.int32, (tile, slab_rows), 1) + lane * slab_rows
-            chosen = (place[at, :] == spots).astype(jnp.bfloat16)
-            term = jnp.dot(chosen, source, preferred_element_type=jnp.float32)
-            if not first:
-                term = total[at, :] + term
-            if final:
-                out[at, :] = term.astype(jnp.bfloat16)
-            else:
-                total[at, :] = term
-            return carry
-
-        lax.fori_loop(0, capacity // tile, one_tile, 0)
-
-    put(1, leaving[1], True, False)
+    arrived[1] = spread(1)
     for lane in (2, 0, 3):
         lane_copy(lane).wait()
-        put(lane, arrived[lane], False, lane == 3)
 
     for step in range(1, parts):
         window_copy(step).wait_send()
@@ -339,21 +331,18 @@
             tail_copy(step).wait_send()
 
 
-def leave(index, place, result, bricks, lanes, slab_rows):
+def leave(index, result, bricks, lanes, slab_rows):
     parts, quarter, width = result.shape
     rows = index.shape[1]
-    capacity = place.shape[0]
     whole = pl.BlockSpec(memory_space=pltpu.VMEM)
     return pl.pallas_call(
         functools.partial(leave_kernel, bricks, parts),
-        out_shape=jax.ShapeDtypeStruct((capacity, width), jnp.bfloat16),
-        in_specs=[whole, whole, whole],
+        out_shape=jax.ShapeDtypeStruct((lanes, slab_rows, width), jnp.bfloat16),
+        in_specs=[whole, whole],
         out_specs=whole,
         scratch_shapes=[
             pltpu.VMEM((rows, width), jnp.bfloat16),
             pltpu.VMEM((lanes, slab_rows, width), jnp.bfloat16),
-            pltpu.VMEM((lanes, slab_rows, width), jnp.bfloat16),
-            pltpu.VMEM((capacity, width), jnp.float32),
             pltpu.SemaphoreType.DMA((parts,)),
             pltpu.SemaphoreType.DMA((parts,)),
             pltpu.SemaphoreType.DMA((parts,)),
@@ -365,11 +354,77 @@
             collective_id=1, has_side_effects=True, vmem_limit_bytes=VMEM_BYTES
         ),
         cost_estimate=pl.CostEstimate(
-            flops=4 * rows * lanes * slab_rows * width,
+            flops=2 * rows * lanes * slab_rows * width,
             bytes_accessed=20 * slab_rows * width * lanes,
             transcendentals=0,
         ),
-    )(index, place, result)
+    )(index, result)
+
+
+def cut_kernel(starts, voxel_feats, slabs, held, arrived):
+    part = lax.axis_index("mp")
+    lanes, slab_rows, width = slabs.shape
+    held_rows = held.shape[1]
+
+    def copy(lane):
+        first = pl.multiple_of(starts[1, lane], ALIGN)
+        column = pl.multiple_of(part * width, width)
+        return pltpu.make_async_copy(
+            voxel_feats.at[pl.ds(first, held_rows), pl.ds(column, width)],
+            held.at[lane],
+            arrived.at[lane],
+        )
+
+    for lane in range(lanes):
+        copy(lane).start()
+    for lane in range(lanes):
+        copy(lane).wait()
+        rows = held[lane].astype(jnp.float32)
+        ahead = starts[0, lane] - starts[1, lane]
+        turned = pltpu.roll(rows, lax.rem(held_rows - ahead, held_rows), 0)
+        slabs[lane] = turned[:slab_rows].astype(jnp.bfloat16)
+
+
+def cut(starts, voxel_feats, slab_rows, parts):
+    lanes = starts.shape[1]
+    width = voxel_feats.shape[1] // parts
+    return pl.pallas_call(
+        cut_kernel,
+        out_shape=jax.ShapeDtypeStruct((lanes, slab_rows, width), jnp.bfloat16),
+        in_specs=[pl.BlockSpec(memory_space=pltpu.SMEM), pl.BlockSpec(memory_space=pl.ANY)],
+        out_specs=pl.BlockSpec(memory_space=pltpu.VMEM),
+        scratch_shapes=[
+            pltpu.VMEM((lanes, slab_rows + ALIGN, width), jnp.bfloat16),
+            pltpu.SemaphoreType.DMA((lanes,)),
+        ],
+        compiler_params=pltpu.CompilerParams(vmem_limit_bytes=VMEM_BYTES),
+    )(starts, voxel_feats)
+
+
+def place_kernel(starts, slabs, out, total):
+    lanes, slab_rows, width = slabs.shape
+    total[...] = jnp.zeros_like(total)
+    for lane in range(lanes):
+        rows = jnp.concatenate(
+            [slabs[lane].astype(jnp.float32), jnp.zeros((ALIGN, width), jnp.float32)], axis=0
+        )
+        turned = pltpu.roll(rows, starts[0, lane] - starts[1, lane], 0)
+        at = pl.ds(pl.multiple_of(starts[1, lane], ALIGN), slab_rows + ALIGN)
+        total[at, :] += turned
+    out[...] = total[...].astype(jnp.bfloat16)
+
+
+def place(starts, slabs, capacity):
+    width = slabs.shape[2]
+    whole = pl.BlockSpec(memory_space=pltpu.VMEM)
+    return pl.pallas_call(
+        place_kernel,
+        out_shape=jax.ShapeDtypeStruct((capacity, width), jnp.bfloat16),
+        in_specs=[pl.BlockSpec(memory_space=pltpu.SMEM), whole],
+        out_specs=whole,
+        scratch_shapes=[pltpu.VMEM((capacity, width), jnp.float32)],
+        compiler_params=pltpu.CompilerParams(vmem_limit_bytes=VMEM_BYTES),
+    )(starts, slabs)
 
 
 def layer_norm(values, gain):
@@ -390,8 +445,16 @@
     queries,
     keys,
     values,
+    held,
+    arrived,
 ):
     groups, _, triple = weights.shape
+
+    def copy(group):
+        return pltpu.make_async_copy(weights.at[group], held.at[group], arrived.at[group])
+
+    for group in range(groups):
+        copy(group).start()
     lanes = triple // 3
     group_heads = lanes // head_dim
     query_rows = attended.shape[0]
@@ -400,7 +463,8 @@
     scale = head_dim ** (-0.5) * math.log2(math.e)
     lane_head = lax.broadcasted_iota(jnp.int32, (1, lanes), 1) // head_dim
     for group in range(groups):
-        weight = weights[group]
+        copy(group).wait()
+        weight = held[group]
         queries[group] = (
             jnp.dot(
                 normed[pl.ds(start, query_rows), :],
@@ -461,13 +525,20 @@
     return pl.pallas_call(
         functools.partial(attention_kernel, head_dim, query_rows),
         out_shape=jax.ShapeDtypeStruct((query_rows, groups * lanes), jnp.bfloat16),
-        in_specs=[pl.BlockSpec(memory_space=pltpu.SMEM), whole, whole, whole],
+        in_specs=[
+            pl.BlockSpec(memory_space=pltpu.SMEM),
+            whole,
+            whole,
+            pl.BlockSpec(memory_space=pl.ANY),
+        ],
         out_specs=whole,
         scratch_shapes=[
             pltpu.VMEM((rows, width), jnp.bfloat16),
             pltpu.VMEM((groups, query_rows, lanes), jnp.bfloat16),
             pltpu.VMEM((groups, rows, lanes), jnp.bfloat16),
             pltpu.VMEM((groups, rows, 2 * lanes), jnp.bfloat16),
+            pltpu.VMEM(weights.shape, jnp.bfloat16),
+            pltpu.SemaphoreType.DMA((groups,)),
         ],
         compiler_params=pltpu.CompilerParams(vmem_limit_bytes=VMEM_BYTES),
         cost_estimate=pl.CostEstimate(
@@ -565,22 +636,19 @@
     qkv_sorted = jnp.dot(
         qkv_weight, shuffle, preferred_element_type=jnp.float32
     ).astype(jnp.bfloat16)
-    qkv_all = lax.all_gather(qkv_sorted, "mp", axis=0)
-    mlp_all = lax.all_gather(
-        jnp.concatenate([proj_weight, up_weight, down_weight], axis=0), "mp", axis=0
+    qkv_half = gathered(qkv_sorted[None], "far")
+    mlp_half = gathered(
+        jnp.concatenate([proj_weight, up_weight, down_weight], axis=0)[None], "far"
     )
 
     lane_ids = jnp.arange(4, dtype=jnp.int32)
     lane_targets = wrapped(my_index - (lane_ids - 1), bricks)
     low = lane_targets * shard_rows
     below = slot_rank[:, None] < low[None, :]
-    upto = slot_rank[:, None] < (low + shard_rows)[None, :]
     run_starts = jnp.sum(below.astype(jnp.int32), axis=0)
     slab_starts = jnp.minimum(run_starts, latest)
-    in_run = jnp.logical_and(upto, jnp.logical_not(below))
-    slot_ids = jnp.arange(capacity, dtype=jnp.int32)
-    spots = slot_ids[:, None] + (lane_ids * pair_rows - slab_starts)[None, :] + 1
-    place = jnp.sum(jnp.where(in_run, spots, 0), axis=1, keepdims=True) - 1
+    aligned = jnp.minimum(slab_starts // ALIGN * ALIGN, latest - ALIGN)
+    starts = jnp.stack([slab_starts, aligned])
 
     source_brick = curve_order // capacity
     source_slot = curve_order - source_brick * capacity
@@ -594,21 +662,19 @@
         jnp.concatenate([empty, recv_index, empty]), offset, shard_rows + PATCH, 0
     )
 
-    column = (part_index * width_part).astype(jnp.uint32)
-    starts = slab_starts.astype(jnp.uint32)
-    slabs = jnp.stack(
-        [
-            lax.dynamic_slice(voxel_feats, (starts[lane], column), (pair_rows, width_part))
-            for lane in range(4)
-        ]
-    )
-    patch_rows = enter(index[:, None], slabs, bricks, model_parts)
+    slabs = cut(starts, voxel_feats, pair_rows, model_parts)
+    qkv_half, slabs = lax.optimization_barrier((qkv_half, slabs))
+    qkv_all = gathered(qkv_half, "near")
+    patch_rows = enter(index[None, :], slabs, bricks, model_parts)
+    mlp_half, patch_rows = lax.optimization_barrier((mlp_half, patch_rows))
+    mlp_all = gathered(mlp_half, "near")
     query_from = (lax.rem(part_index * quarter_rows, PATCH))[None]
     attended = attention(
         patch_rows, norm_gains[0:1], qkv_all, query_from, quarter_rows, head_dim
     )
     result = mlp(patch_rows, attended, norm_gains[1:2], mlp_all, query_from)
-    return leave(index[None, :], place, result, bricks, 4, pair_rows)
+    returned = leave(index[None, :], result, bricks, 4, pair_rows)
+    return place(starts, returned, capacity)
 
 
 def solution(mesh):

time: 187 us -> 169 us (0.904)
  Pallas kernels: 152 us -> 131 us
  blocking collectives: 0 us -> 14.3 us
  local copies, waits for them, and re-layouts: 14.9 us -> 3.66 us
    pallas_call x1, Pallas kernels: 59.6 us -> 44.3 us  [enter(): pl.pallas_call(functools.partial(enter_kernel, bricks, parts), out_shape=...]
    all_gather x0 -> x1, blocking collectives: none -> 14.3 us  [gathered(): lax.all_gather(value, 'mp', axis=0, tiled=True, axis_index_groups=groups)]
    pallas_call x1, Pallas kernels: 48.9 us -> 36.3 us  [leave(): pl.pallas_call(functools.partial(leave_kernel, bricks, parts), out_shape=...]
    pallas_call x0 -> x2, Pallas kernels: none -> 6.59 us  [the longest x1 3.5 us: cut(): pl.pallas_call(cut_kernel, out_shape=jax.ShapeDtypeStruct((lanes, slab_ro...]
    another operation x1 -> x0, local copies, waits for them, and re-layouts: 4.51 us -> none  [per_device(): jnp.stack([lax.dynamic_slice(voxel_feats, (starts[lane], column), (pair_r...]
    unnamed x15 -> x8, local copies, waits for them, and re-layouts: 3.06 us -> 0.64 us
    all_gather x1, local copies, waits for them, and re-layouts: 2.66 us -> 0.57 us  [gathered(): lax.all_gather(value, 'mp', axis=0, tiled=True, axis_index_groups=groups)]
  transfers between devices with their start and end apart: 2 -> 3, of which waited for: 0 -> 0; matrix products, arithmetic and copies ran while one was open for 8% -> 3% of each run, Pallas kernels for 52% -> 51%
where the time goes in v3:
time: 169 us; the launch traced here: 168 us
  Pallas kernels  131 us (78%)
  blocking collectives  14.3 us (8%)
  between operations  13.9 us (8%)
  other arithmetic  4.1 us (2%)
  local copies, waits for them, and re-layouts  3.66 us (2%)
    pallas_call x1, Pallas kernels, enter(): pl.pallas_call(functools.partial(enter_kernel, bricks, parts), out_shape=...  44.3 us
    pallas_call x1, Pallas kernels, attention(): pl.pallas_call(functools.partial(attention_kernel, head_dim, query_rows),...  37.3 us
    pallas_call x1, Pallas kernels, leave(): pl.pallas_call(functools.partial(leave_kernel, bricks, parts), out_shape=...  36.3 us
    all_gather x1, blocking collectives, gathered(): lax.all_gather(value, 'mp', axis=0, tiled=True, axis_index_groups=groups)  14.3 us
    pallas_call x1, Pallas kernels, mlp(): pl.pallas_call(mlp_kernel, out_shape=jax.ShapeDtypeStruct((groups, rows,...  7.01 us
    pallas_call x1, Pallas kernels, cut(): pl.pallas_call(cut_kernel, out_shape=jax.ShapeDtypeStruct((lanes, slab_ro...  3.5 us
  transfers between devices with their start and end apart: 3, of which 0 were waited for; matrix products, arithmetic and copies ran while one was open for 3% of the time, Pallas kernels for 51%

profile of v3, /device:TPU:0, one launch (start us, length us, event | category | flops | bytes accessed | tf_op | source)
XLA Modules:
  0.0 168.0 jit_solution(4521483904144893860)
XLA Ops:
  6.5 0.0 copy-start
  6.5 0.0 all-gather.10.cloned.1.call-start
  6.5 2.4 %pad_maximum_fusion = bf16[1152,512]{1,0:T(8,128)(2,1)} fusion(bf16[512,512]{1,0:T(8,128)(2,1)} %param.16, bf16[512,512]{1,0:T(8,128)(2,1)} %param.15, bf16[128,512]{1,0:T(8,128)(2,1)} %param.14), kind=kLoop, calls=%fused_computation.2 | loop fusion | flops 3538944 | bytes 2359296 | tf_op jit(solution)/shard_map/concatenate | solution.py:641
  8.9 0.0 copy-start.2
  8.9 0.0 all-gather.10.cloned.1.call-update
  8.9 0.0 all-gather.6.cloned.1.call-start
  9.0 0.0 copy-done
  9.0 0.4 fusion
  9.4 14.3 %all-gather.1 = bf16[1024,384]{0,1:T(8,128)(2,1)S(1)} all-gather(bf16[512,384]{0,1:T(8,128)(2,1)S(1)} %fusion), channel_id=3, replica_groups={{0,2},{1,3},{4,6},{5,7},{8,10},{9,11},{12,14},{13,15},{16,18},{17,19},{..., dimensions={0}, use_global_device_ids=true | all-gather | bytes 1179648 | tf_op jit(solution)/shard_map/all_gather | solution.py:28
  23.7 0.6 reshape.132
  24.3 0.0 copy-done.2
  24.3 0.2 convert_reduce_fusion
  24.5 0.5 pad_add_fusion.starts
  25.1 0.0 copy-start.1
  25.1 3.5 %shard_map.91.slabs = bf16[4,768,128]{2,1,0:T(8,128)(2,1)} custom-call(s32[2,4]{1,0:T(2,128)} %pad_add_fusion.starts, bf16[3072,512]{1,0:T(8,128)(2,1)} %voxel_feats.1), custom_call_target="tpu_custom_call" | custom-call | tf_op jit(solution)/shard_map/pallas_call | solution.py:391
  28.6 1.9 %copy.12 = bf16[2,512,384]{2,1,0:T(8,128)(2,1)} copy(bf16[2,512,384]{1,0,2:T(2,128)(2,1)S(1)} %reshape.132) | data formatting | bytes 1572864 | tf_op jit(solution)/shard_map/optimization_barrier | solution.py:666
  30.4 0.0 all-gather.6.cloned.1.call-update
  30.5 0.0 all-gather.8.cloned.1.call-start
  31.2 0.0 copy-done.1
  31.2 0.1 select_reduce_fusion.1
  31.3 0.1 select_reduce_fusion
  31.4 0.7 fusion.5
  32.1 44.3 %shard_map.92.patch_rows = bf16[1024,512]{1,0:T(8,128)(2,1)} custom-call(s32[1,3072]{1,0:T(1,128)} %bitcast.14, bf16[4,768,128]{2,1,0:T(8,128)(2,1)} %shard_map.91.slabs), custom_call_target="tpu_custom_call" | custom-call | flops 2415919104 | bytes 7864320 | tf_op jit(solution)/shard_map/pallas_call | solution.py:185
  76.5 0.0 copy-start.3
  76.5 0.0 all-gather.10.cloned.1.call-done
  76.5 0.0 all-gather.8.cloned.1.call-update
  76.5 0.6 copy-done.3
  77.1 0.6 fusion.21
  77.7 0.0 all-gather.6.cloned.1.call-done.weights
  77.7 37.3 %shard_map.93.attended = bf16[512,512]{1,0:T(8,128)(2,1)} custom-call(s32[1]{0:T(128)} %bitcast.3.query_from, bf16[1024,512]{1,0:T(8,128)(2,1)} %shard_map.92.patch_rows, f32[1,512]{1,0:T(1,128)} %get-tuple-element.16.gain, bf16[4,512,384]{2,1,0:T(8,128)(2,1)} %all-gather.6.cloned.1.call-done.weights), custom_call_target="tpu_custom_call" | custom-call | flops 17179869184 | bytes 2097152 | tf_op jit(solution)/shard_map/pallas_call | solution.py:525
  115.1 0.0 all-gather.8.cloned.1.call-done.weights
  115.1 7.0 %shard_map.94.result = bf16[4,512,128]{2,1,0:T(8,128)(2,1)} custom-call(s32[1]{0:T(128)} %bitcast.3.query_from, bf16[1024,512]{1,0:T(8,128)(2,1)} %shard_map.92.patch_rows, bf16[512,512]{1,0:T(8,128)(2,1)} %shard_map.93.attended, f32[1,512]{1,0:T(1,128)} %get-tuple-element.15.gain, bf16[4,1152,512]{2,1,0:T(8,128)(2,1)} %all-gather.8.cloned.1.call-done.weights), custom_call_target="tpu_custom_call" | custom-call | flops 2147483648 | bytes 8388608 | tf_op jit(solution)/shard_map/pallas_call | solution.py:592
  122.1 36.3 %shard_map.95.slabs = bf16[4,768,128]{2,1,0:T(8,128)(2,1)} custom-call(s32[1,3072]{1,0:T(1,128)} %bitcast.15, bf16[4,512,128]{2,1,0:T(8,128)(2,1)} %shard_map.94.result), custom_call_target="tpu_custom_call" | custom-call | flops 2415919104 | bytes 7864320 | tf_op jit(solution)/shard_map/pallas_call | solution.py:338
  158.4 3.1 %shard_map.96 = bf16[3072,128]{1,0:T(8,128)(2,1)} custom-call(s32[2,4]{1,0:T(2,128)} %pad_add_fusion.starts, bf16[4,768,128]{2,1,0:T(8,128)(2,1)} %shard_map.95.slabs), custom_call_target="tpu_custom_call" | custom-call | tf_op jit(solution)/shard_map/pallas_call | solution.py:420
  (7 shorter events, 0.1 us)
Async XLA Ops:
  6.5 2.5 %copy-start = (bf16[512,384]{1,0:T(8,128)(2,1)S(1)}, bf16[512,384]{1,0:T(8,128)(2,1)}, u32[]{:S(2)}) copy-start(bf16[512,384]{1,0:T(8,128)(2,1)} %param.13) | copy-start | bytes 1179652
  6.5 70.0 %all-gather.10.cloned.1.call-start = ((), (), s32[]{:S(2)}) async-start(), calls=%async_computation.2 | async-start | bytes 3538944 | tf_op jit(solution)/shard_map/all_gather | solution.py:28
  8.9 15.4 %copy-start.2 = (s32[3072]{0:T(1024)S(1)}, s32[3072]{0:T(1024)}, u32[]{:S(2)}) copy-start(s32[3072]{0:T(1024)} %param.10) | copy-start | bytes 36868
  8.9 68.8 %all-gather.6.cloned.1.call-start = ((), (), s32[]{:S(2)}) async-start(), calls=%async_computation | async-start | bytes 2359296 | tf_op jit(solution)/shard_map/all_gather | solution.py:28
  25.1 6.1 %copy-start.1 = (s32[2048]{0:T(1024)S(1)}, s32[2048]{0:T(1024)}, u32[]{:S(2)}) copy-start(s32[2048]{0:T(1024)} %param.11) | copy-start | bytes 24580
  30.5 84.6 %all-gather.8.cloned.1.call-start = ((), (), s32[]{:S(2)}) async-start(), calls=%async_computation.1 | async-start | bytes 7077888 | tf_op jit(solution)/shard_map/all_gather | solution.py:28
  76.5 0.7 copy-start.3
Sparse Core Ops, SparseCore 0:
  9.1 38.7 all-gather.9
  49.4 11.1 all-gather.5
  76.6 18.7 all-gather.7

commit v4 on v3

--- a/solution.py
+++ b/solution.py
@@ -18,14 +18,15 @@
 MESH = pl.DeviceIdType.MESH
 
 
-def gathered(value, reach):
+def passed(value, patches, patch_step, near_step):
     parts = lax.axis_size("mp")
-    half = parts // 2
-    if reach == "far":
-        groups = [[first, first + half] for first in range(half)]
-    else:
-        groups = [list(range(half)), list(range(half, parts))]
-    return lax.all_gather(value, "mp", axis=0, tiled=True, axis_index_groups=groups)
+    half = parts // patches
+    pairs = []
+    for source in range(parts):
+        patch, place = source // half, source % half
+        target = (patch + patch_step) % patches * half + (place + near_step) % half
+        pairs.append((source, target))
+    return lax.ppermute(value, "mp", pairs)
 
 
 def wrapped(value, count):
@@ -33,11 +34,11 @@
     return jnp.where(value >= count, value - count, value)
 
 
-def greet_all(bricks, parts):
+def greet_all(bricks, parts, wide):
     brick, part = lax.axis_index("brick"), lax.axis_index("mp")
     barrier = pltpu.get_barrier_semaphore()
     peers = [(0, step) for step in range(1, parts)]
-    peers += [(away, step) for away in (-1, 1) for step in range(parts)]
+    peers += [(away, step) for away in (-1, 1) for step in range(parts if wide else 1)]
     peers += [(-2, 0), (2, 0)]
     for away, step in peers:
         pl.semaphore_signal(
@@ -63,8 +64,10 @@
     column_index,
     lane_send,
     lane_recv,
-    window_send,
-    window_recv,
+    far_send,
+    far_recv,
+    near_send,
+    near_recv,
     head_send,
     head_recv,
 ):
@@ -73,8 +76,7 @@
     rows = index.shape[1]
     tile = 1024
     lane_width = column_index.shape[1]
-    quarter = (rows - PATCH) // parts
-    greet_all(bricks, parts)
+    greet_all(bricks, parts, False)
 
     def lane_copy(lane):
         return pltpu.make_async_remote_copy(
@@ -120,62 +122,84 @@
         merge(lane, arrived[lane], False)
     merged[...] = total[...].astype(jnp.bfloat16)
 
-    def patch_start(target):
-        return pl.multiple_of((target * quarter // PATCH + 1) * PATCH, PATCH)
-
-    last = rows - PATCH
-
-    def head_copy(step):
-        target = lax.rem(part + step, parts)
+    patches = (rows - PATCH) // PATCH
+    half = parts // patches
+    patch, place = part // half, lax.rem(part, half)
+    last = patches - 1
+
+    def rows_of(which):
+        return pl.ds(pl.multiple_of((which + 1) * PATCH, PATCH), PATCH)
+
+    head_copy = pltpu.make_async_remote_copy(
+        src_ref=merged.at[pl.ds(0, PATCH)],
+        dst_ref=head_in,
+        send_sem=head_send.at[0],
+        recv_sem=head_recv.at[0],
+        device_id=(lax.rem(brick - 1 + bricks, bricks), part),
+        device_id_type=MESH,
+    )
+    head_copy.start()
+
+    def far_target(step):
+        return lax.rem(patch + step, patches)
+
+    def far_copy(step):
         return pltpu.make_async_remote_copy(
-            src_ref=merged.at[pl.ds(0, PATCH)],
-            dst_ref=head_in.at[step],
-            send_sem=head_send.at[step],
-            recv_sem=head_recv.at[step],
-            device_id=(lax.rem(brick - 1 + bricks, bricks), target),
-            device_id_type=MESH,
-        )
-
-    def window_copy(step):
-        target = lax.rem(part + step, parts)
+            src_ref=merged.at[rows_of(far_target(step))],
+            dst_ref=window_in.at[part],
+            send_sem=far_send.at[step],
+            recv_sem=far_recv.at[step],
+            device_id=(brick, far_target(step) * half + place),
+            device_id_type=MESH,
+        )
+
+    def near_copy(step, far_step):
+        source = lax.rem(patch - far_step + patches, patches) * half + place
         return pltpu.make_async_remote_copy(
-            src_ref=merged.at[pl.ds(patch_start(target), PATCH)],
-            dst_ref=window_in.at[step],
-            send_sem=window_send.at[step],
-            recv_sem=window_recv.at[step],
-            device_id=(brick, target),
-            device_id_type=MESH,
-        )
-
-    for step in range(parts):
-
-        @pl.when(patch_start(lax.rem(part + step, parts)) == last)
-        def _():
-            head_copy(step).start()
-
-    for step in range(1, parts):
-        window_copy(step).start()
-
-    def columns(step):
-        source = lax.rem(part - step + parts, parts)
-        return pl.ds(pl.multiple_of(source * width, width), width)
-
-    patch_rows[:, columns(0)] = merged[pl.ds(patch_start(part), PATCH), :]
-    for step in range(1, parts):
-        window_copy(step).wait()
-        patch_rows[:, columns(step)] = window_in[step]
-
-    @pl.when(patch_start(part) == last)
+            src_ref=window_in.at[source],
+            dst_ref=window_in.at[source],
+            send_sem=near_send.at[step, far_step],
+            recv_sem=near_recv.at[step, far_step],
+            device_id=(brick, patch * half + lax.rem(place + step, half)),
+            device_id_type=MESH,
+        )
+
+    def start_far(late):
+        for step in range(1, patches):
+
+            @pl.when((far_target(step) == last) if late else (far_target(step) != last))
+            def _():
+                far_copy(step).start()
+
+    def start_own():
+        window_in[part] = merged[rows_of(patch), :]
+        for step in range(1, half):
+            near_copy(step, 0).start()
+
+    start_far(False)
+
+    @pl.when(patch != last)
     def _():
-        for step in range(parts):
-            head_copy(step).wait_recv()
-            patch_rows[:, columns(step)] += head_in[step]
-
-    for step in range(parts):
-
-        @pl.when(patch_start(lax.rem(part + step, parts)) == last)
-        def _():
-            head_copy(step).wait_send()
+        start_own()
+
+    head_copy.wait_recv()
+    merged[rows - PATCH :, :] += head_in[...]
+    start_far(True)
+
+    @pl.when(patch == last)
+    def _():
+        start_own()
+
+    for far_step in range(1, patches):
+        far_copy(far_step).wait()
+        for step in range(1, half):
+            near_copy(step, far_step).start()
+    for far_step in range(patches):
+        for step in range(1, half):
+            near_copy(step, far_step).wait()
+    head_copy.wait_send()
+    for source in range(parts):
+        patch_rows[:, source * width : (source + 1) * width] = window_in[source]
 
 
 def enter(index, slabs, bricks, parts):
@@ -192,14 +216,16 @@
             pltpu.VMEM((rows, width), jnp.float32),
             pltpu.VMEM((rows, width), jnp.bfloat16),
             pltpu.VMEM((parts, PATCH, width), jnp.bfloat16),
-            pltpu.VMEM((parts, PATCH, width), jnp.bfloat16),
+            pltpu.VMEM((PATCH, width), jnp.bfloat16),
             pltpu.VMEM((rows, 128), jnp.int32),
             pltpu.SemaphoreType.DMA((lanes,)),
             pltpu.SemaphoreType.DMA((lanes,)),
             pltpu.SemaphoreType.DMA((parts,)),
             pltpu.SemaphoreType.DMA((parts,)),
-            pltpu.SemaphoreType.DMA((parts,)),
-            pltpu.SemaphoreType.DMA((parts,)),
+            pltpu.SemaphoreType.DMA((parts, parts)),
+            pltpu.SemaphoreType.DMA((parts, parts)),
+            pltpu.SemaphoreType.DMA((1,)),
+            pltpu.SemaphoreType.DMA((1,)),
         ],
         compiler_params=pltpu.CompilerParams(
             collective_id=0, has_side_effects=True, vmem_limit_bytes=VMEM_BYTES
@@ -220,6 +246,7 @@
     arrived,
     rows_in,
     leaving,
+    total,
     window_send,
     window_recv,
     tail_send,
@@ -232,7 +259,7 @@
     quarter = result.shape[1]
     rows = rows_in.shape[0]
     last = rows - PATCH
-    greet_all(bricks, parts)
+    greet_all(bricks, parts, True)
 
     def row_start(source):
         return PATCH + source * quarter
@@ -294,10 +321,6 @@
     rows_in[pl.ds(pl.multiple_of(row_start(part), quarter), quarter), :] = result[part]
     for step in range(1, parts):
         window_arrival(step).wait_recv()
-    for source in range(parts):
-        if row_start(source) >= last:
-            tail_arrival(source).wait_recv()
-
     def lane_copy(lane):
         return pltpu.make_async_remote_copy(
             src_ref=leaving.at[lane],
@@ -308,17 +331,22 @@
             device_id_type=MESH,
         )
 
-    def spread(lane):
-        spots = lax.broadcasted_iota(jnp.int32, (slab_rows, rows), 0) + lane * slab_rows
-        chosen = jnp.where(index[...] == spots, 1.0, 0.0).astype(jnp.bfloat16)
-        return jnp.dot(
-            chosen, rows_in[...], preferred_element_type=jnp.float32
+    def spread(lane, start, stop):
+        spots = lax.broadcasted_iota(jnp.int32, (slab_rows, stop - start), 0)
+        chosen = jnp.where(
+            index[:, start:stop] == spots + lane * slab_rows, 1.0, 0.0
         ).astype(jnp.bfloat16)
-
+        return jnp.dot(chosen, rows_in[start:stop, :], preferred_element_type=jnp.float32)
+
+    for lane in range(lanes):
+        total[lane] = spread(lane, PATCH, rows)
+    for source in range(parts):
+        if row_start(source) >= last:
+            tail_arrival(source).wait_recv()
     for lane in (3, 0, 2):
-        leaving[lane] = spread(lane)
+        leaving[lane] = (total[lane] + spread(lane, 0, PATCH)).astype(jnp.bfloat16)
         lane_copy(lane).start()
-    arrived[1] = spread(1)
+    arrived[1] = (total[1] + spread(1, 0, PATCH)).astype(jnp.bfloat16)
     for lane in (2, 0, 3):
         lane_copy(lane).wait()
 
@@ -343,6 +371,7 @@
         scratch_shapes=[
             pltpu.VMEM((rows, width), jnp.bfloat16),
             pltpu.VMEM((lanes, slab_rows, width), jnp.bfloat16),
+            pltpu.VMEM((lanes, slab_rows, width), jnp.float32),
             pltpu.SemaphoreType.DMA((parts,)),
             pltpu.SemaphoreType.DMA((parts,)),
             pltpu.SemaphoreType.DMA((parts,)),
@@ -446,13 +475,17 @@
     keys,
     values,
     held,
+    mixed,
     arrived,
 ):
-    groups, _, triple = weights.shape
+    groups, depth, triple = held.shape
 
     def copy(group):
-        return pltpu.make_async_copy(weights.at[group], held.at[group], arrived.at[group])
-
+        return pltpu.make_async_copy(
+            weights.at[pl.ds(group * depth, depth)], held.at[group], arrived.at[group]
+        )
+
+    mixed[...] = jnp.zeros_like(mixed)
     for group in range(groups):
         copy(group).start()
     lanes = triple // 3
@@ -480,50 +513,57 @@
         values[group, :, :lanes] = both[:, lanes:]
         values[group, :, lanes:] = jnp.ones_like(both[:, lanes:])
 
-    def one_group(group, carry):
-        attended_group = [
-            jnp.zeros((query_tile, lanes), jnp.float32)
-            for _ in range(query_rows // query_tile)
-        ]
-
-        def one_head(head, sums):
-            mine = lane_head == head
-            results = []
-            for tile in range(query_rows // query_tile):
-                query = queries[group, tile * query_tile : (tile + 1) * query_tile, :]
-                query = jnp.where(mine, query, jnp.zeros_like(query))
-                scores = lax.dot_general(
-                    query,
-                    keys[group],
-                    (((1,), (1,)), ((), ())),
-                    preferred_element_type=jnp.float32,
-                )
-                highest = jnp.max(scores, axis=-1, keepdims=True)
-                exps = jnp.exp2((scores - highest).astype(jnp.bfloat16))
-                product = jnp.dot(
-                    exps, values[group], preferred_element_type=jnp.float32
-                )
-                result = product[:, :lanes] / product[:, lanes:]
-                results.append(jnp.where(mine, result, sums[tile]))
-            return tuple(results)
-
-        sums = lax.fori_loop(0, group_heads, one_head, tuple(attended_group), unroll=2)
-        for tile in range(query_rows // query_tile):
-            attended[tile * query_tile : (tile + 1) * query_tile, pl.ds(
-                pl.multiple_of(group * lanes, lanes), lanes
-            )] = sums[tile].astype(jnp.bfloat16)
+    heads_once = 4
+    chunks = query_rows // query_tile
+
+    def some_heads(turn, carry):
+        group = turn // (group_heads // heads_once)
+        first_head = lax.rem(turn, group_heads // heads_once) * heads_once
+        work = [(head, chunk) for head in range(heads_once) for chunk in range(chunks)]
+
+        def rows_at(chunk):
+            return slice(chunk * query_tile, (chunk + 1) * query_tile)
+
+        def score(head, chunk):
+            query = queries[group, rows_at(chunk), :]
+            query = jnp.where(lane_head == first_head + head, query, jnp.zeros_like(query))
+            return lax.dot_general(
+                query,
+                keys[group],
+                (((1,), (1,)), ((), ())),
+                preferred_element_type=jnp.float32,
+            )
+
+        def finish(head, chunk, exps):
+            product = jnp.dot(exps, values[group], preferred_element_type=jnp.float32)
+            result = product[:, :lanes] / product[:, lanes:]
+            mine = lane_head == first_head + head
+            at = rows_at(chunk)
+            mixed[group, at, :] = jnp.where(mine, result, mixed[group, at, :])
+
+        scores, exps = score(*work[0]), None
+        for step, item in enumerate(work):
+            later = score(*work[step + 1]) if step + 1 < len(work) else None
+            highest = jnp.max(scores, axis=-1, keepdims=True)
+            now = jnp.exp2((scores - highest).astype(jnp.bfloat16))
+            if step:
+                finish(*work[step - 1], exps)
+            scores, exps = later, now
+        finish(*work[-1], exps)
         return carry
 
-    lax.fori_loop(0, groups, one_group, 0)
+    lax.fori_loop(0, groups * group_heads // heads_once, some_heads, 0)
+    for group in range(groups):
+        attended[:, group * lanes : (group + 1) * lanes] = mixed[group].astype(jnp.bfloat16)
 
 
 def attention(patch_rows, gain, weights, query_from, query_rows, head_dim):
-    groups, width, triple = weights.shape
+    rows, width = patch_rows.shape
+    groups, triple = weights.shape[0] // width, weights.shape[1]
     lanes = triple // 3
-    rows = patch_rows.shape[0]
     whole = pl.BlockSpec(memory_space=pltpu.VMEM)
     return pl.pallas_call(
-        functools.partial(attention_kernel, head_dim, query_rows),
+        functools.partial(attention_kernel, head_dim, query_rows // 2),
         out_shape=jax.ShapeDtypeStruct((query_rows, groups * lanes), jnp.bfloat16),
         in_specs=[
             pl.BlockSpec(memory_space=pltpu.SMEM),
@@ -537,7 +577,8 @@
             pltpu.VMEM((groups, query_rows, lanes), jnp.bfloat16),
             pltpu.VMEM((groups, rows, lanes), jnp.bfloat16),
             pltpu.VMEM((groups, rows, 2 * lanes), jnp.bfloat16),
-            pltpu.VMEM(weights.shape, jnp.bfloat16),
+            pltpu.VMEM((groups, width, triple), jnp.bfloat16),
+            pltpu.VMEM((groups, query_rows, lanes), jnp.float32),
             pltpu.SemaphoreType.DMA((groups,)),
         ],
         compiler_params=pltpu.CompilerParams(vmem_limit_bytes=VMEM_BYTES),
@@ -549,20 +590,21 @@
     )(query_from, patch_rows, gain, weights)
 
 
-def mlp_kernel(query_from, patch_rows, attended, gain, weights, result):
-    groups, _, width_full = weights.shape
+def mlp_kernel(scalars, patch_rows, attended, gain, *refs):
+    weights, result = refs[:-1], refs[-1]
+    groups = len(weights)
     rows = attended.shape[0]
     depth = attended.shape[1] // groups
-    hidden_part = (weights.shape[1] - depth) // 2
-    proj_weight = [weights[group, :depth, :] for group in range(groups)]
-    up_weight = [weights[group, depth : depth + hidden_part, :] for group in range(groups)]
-    down_weight = [weights[group, depth + hidden_part :, :] for group in range(groups)]
-    start = pl.multiple_of(query_from[0], rows)
+    hidden_part = (weights[0].shape[0] - depth) // 2
+    proj_weight = [weights[group][:depth, :] for group in range(groups)]
+    up_weight = [weights[group][depth : depth + hidden_part, :] for group in range(groups)]
+    down_weight = [weights[group][depth + hidden_part :, :] for group in range(groups)]
+    start = pl.multiple_of(scalars[0], rows)
     own = patch_rows[pl.ds(start, rows), :].astype(jnp.float32)
     mixed = None
     for group in range(groups):
         term = jnp.dot(
-            attended[:, group * depth : (group + 1) * depth],
+            attended[:, pl.ds(pl.multiple_of(scalars[1 + group] * depth, depth), depth)],
             proj_weight[group],
             preferred_element_type=jnp.float32,
         ).astype(jnp.bfloat16).astype(jnp.float32)
@@ -585,14 +627,14 @@
         result[part] = final[:, part * width : (part + 1) * width]
 
 
-def mlp(patch_rows, attended, gain, weights, query_from):
+def mlp(patch_rows, attended, gain, weights, scalars):
     whole = pl.BlockSpec(memory_space=pltpu.VMEM)
     rows, width = attended.shape
-    groups, hidden = weights.shape[0], weights.shape[2]
+    groups, hidden = len(weights), weights[0].shape[1]
     return pl.pallas_call(
         mlp_kernel,
         out_shape=jax.ShapeDtypeStruct((groups, rows, width // groups), jnp.bfloat16),
-        in_specs=[pl.BlockSpec(memory_space=pltpu.SMEM)] + [whole] * 4,
+        in_specs=[pl.BlockSpec(memory_space=pltpu.SMEM)] + [whole] * (3 + groups),
         out_specs=whole,
         compiler_params=pltpu.CompilerParams(vmem_limit_bytes=VMEM_BYTES),
         cost_estimate=pl.CostEstimate(
@@ -600,7 +642,7 @@
             bytes_accessed=8 * width * hidden * groups,
             transcendentals=rows * hidden * groups,
         ),
-    )(query_from, patch_rows, attended, gain, weights)
+    )(scalars, patch_rows, attended, gain, *weights)
 
 
 def per_device(
@@ -636,10 +678,11 @@
     qkv_sorted = jnp.dot(
         qkv_weight, shuffle, preferred_element_type=jnp.float32
     ).astype(jnp.bfloat16)
-    qkv_half = gathered(qkv_sorted[None], "far")
-    mlp_half = gathered(
-        jnp.concatenate([proj_weight, up_weight, down_weight], axis=0)[None], "far"
-    )
+    qkv_all = lax.all_gather(qkv_sorted, "mp", axis=0, tiled=True)
+    patches = shard_rows // PATCH
+    half = model_parts // patches
+    held = jnp.concatenate([proj_weight, up_weight, down_weight], axis=0)
+    far = [held] + [passed(held, patches, step, 0) for step in range(1, patches)]
 
     lane_ids = jnp.arange(4, dtype=jnp.int32)
     lane_targets = wrapped(my_index - (lane_ids - 1), bricks)
@@ -663,16 +706,22 @@
     )
 
     slabs = cut(starts, voxel_feats, pair_rows, model_parts)
-    qkv_half, slabs = lax.optimization_barrier((qkv_half, slabs))
-    qkv_all = gathered(qkv_half, "near")
     patch_rows = enter(index[None, :], slabs, bricks, model_parts)
-    mlp_half, patch_rows = lax.optimization_barrier((mlp_half, patch_rows))
-    mlp_all = gathered(mlp_half, "near")
+    *far, patch_rows = lax.optimization_barrier((*far, patch_rows))
+    weights, origins = [], []
+    for near_step in range(half):
+        for patch_step in range(patches):
+            value = far[patch_step]
+            weights.append(passed(value, patches, 0, near_step) if near_step else value)
+            patch = lax.rem(part_index // half + patches - patch_step, patches)
+            place_in = lax.rem(part_index + half - near_step, half)
+            origins.append(patch * half + place_in)
     query_from = (lax.rem(part_index * quarter_rows, PATCH))[None]
     attended = attention(
         patch_rows, norm_gains[0:1], qkv_all, query_from, quarter_rows, head_dim
     )
-    result = mlp(patch_rows, attended, norm_gains[1:2], mlp_all, query_from)
+    scalars = jnp.concatenate([query_from, jnp.stack(origins)])
+    result = mlp(patch_rows, attended, norm_gains[1:2], weights, scalars)
     returned = leave(index[None, :], result, bricks, 4, pair_rows)
     return place(starts, returned, capacity)
 

time: 169 us -> 134 us (0.79)
  Pallas kernels: 131 us -> 109 us
  blocking collectives: 14.3 us -> 0 us
  starting transfers between devices: 0.09 us -> 3.58 us
  other arithmetic: 4.1 us -> 1.78 us
    all_gather x1 -> x0, blocking collectives: 14.3 us -> none  [gathered(): lax.all_gather(value, 'mp', axis=0, tiled=True, axis_index_groups=groups)]
    pallas_call x1, Pallas kernels: 37.3 us -> 27.8 us  [attention(): pl.pallas_call(functools.partial(attention_kernel, head_dim, query_rows /...]
    pallas_call x1, Pallas kernels: 44.3 us -> 35.6 us  [enter(): pl.pallas_call(functools.partial(enter_kernel, bricks, parts), out_shape=...]
    pallas_call x1, Pallas kernels: 36.3 us -> 31.9 us  [leave(): pl.pallas_call(functools.partial(leave_kernel, bricks, parts), out_shape=...]
    ppermute x0 -> x3, starting transfers between devices: none -> 3.58 us  [passed(): return lax.ppermute(value, 'mp', pairs)]
    concatenate x1 -> x0, other arithmetic: 2.37 us -> none  [per_device(): jnp.concatenate([proj_weight, up_weight, down_weight], axis=0)[None]]
    optimization_barrier x1 -> x0, local copies, waits for them, and re-layouts: 1.86 us -> none  [per_device(): qkv_half, slabs = lax.optimization_barrier((qkv_half, slabs))]
  transfers between devices with their start and end apart: 3 -> 4, of which waited for: 0 -> 0; matrix products, arithmetic and copies ran while one was open for 3% -> 2% of each run, Pallas kernels for 51% -> 50%
where the time goes in v4:
time: 134 us; the launch traced here: 133 us
  Pallas kernels  109 us (81%)
  between operations  14.2 us (11%)
  starting transfers between devices  3.58 us (3%)
  local copies, waits for them, and re-layouts  3.29 us (2%)
  other arithmetic  1.78 us (1%)
    pallas_call x1, Pallas kernels, enter(): pl.pallas_call(functools.partial(enter_kernel, bricks, parts), out_shape=...  35.6 us
    pallas_call x1, Pallas kernels, leave(): pl.pallas_call(functools.partial(leave_kernel, bricks, parts), out_shape=...  31.9 us
    pallas_call x1, Pallas kernels, attention(): pl.pallas_call(functools.partial(attention_kernel, head_dim, query_rows /...  27.8 us
    pallas_call x1, Pallas kernels, mlp(): pl.pallas_call(mlp_kernel, out_shape=jax.ShapeDtypeStruct((groups, rows,...  6.99 us
    ppermute x3, starting transfers between devices, passed(): return lax.ppermute(value, 'mp', pairs)  3.58 us
    pallas_call x1, Pallas kernels, cut(): pl.pallas_call(cut_kernel, out_shape=jax.ShapeDtypeStruct((lanes, slab_ro...  3.5 us
    pallas_call x1, Pallas kernels, place(): pl.pallas_call(place_kernel, out_shape=jax.ShapeDtypeStruct((capacity, wi...  3.1 us
  transfers between devices with their start and end apart: 4, of which 0 were waited for; matrix products, arithmetic and copies ran while one was open for 2% of the time, Pallas kernels for 50%

profile of v4, /device:TPU:0, one launch (start us, length us, event | category | flops | bytes accessed | tf_op | source)
XLA Modules:
  0.0 132.9 jit_solution(16343889220364840983)
XLA Ops:
  6.5 0.0 copy-start
  6.5 0.0 copy-start.3
  6.5 0.0 copy-start.1
  6.5 0.0 all-gather.2.cloned.1.call-start
  6.6 1.0 copy-done
  7.5 0.0 copy-start.2
  7.5 1.2 fusion
  8.7 0.0 all-gather.2.cloned.1.call-update
  8.7 0.0 copy-done.3
  8.7 0.0 copy-start.6
  8.8 0.0 copy-done.1
  8.8 0.0 copy-done.2
  8.9 0.0 copy-start.5
  8.9 3.0 %collective-permute-start = (bf16[1152,512]{1,0:T(8,128)(2,1)S(1)}, bf16[1152,512]{1,0:T(8,128)(2,1)}, u32[]{:S(2)}, u32[]{:S(2)}) collective-permute-start(bf16[1152,512]{1,0:T(8,128)(2,1)S(1)} %constant_dynamic-update-slice_fusion.refs_0_), channel_id=1, source_target_pairs={{0,2},{1,3},{2,0},{3,1},{4,6},{5,7},{6,4},{7,5},{8,10},{9,11},{10,... | collective-permute-start | bytes 3538952 | tf_op jit(solution)/shard_map/ppermute | solution.py:29
  12.6 0.0 copy-done.6
  12.6 0.2 convert_reduce_fusion
  12.8 0.6 pad_add_fusion.starts
  13.4 0.0 copy-start.4
  13.4 0.0 copy-start.7
  13.4 3.5 %shard_map.91.slabs = bf16[4,768,128]{2,1,0:T(8,128)(2,1)} custom-call(s32[2,4]{1,0:T(2,128)} %pad_add_fusion.starts, bf16[3072,512]{1,0:T(8,128)(2,1)} %voxel_feats.1), custom_call_target="tpu_custom_call" | custom-call | tf_op jit(solution)/shard_map/pallas_call | solution.py:420
  16.9 0.6 concatenate.10.scalars
  17.5 0.0 copy-done.4
  17.5 0.1 select_reduce_fusion.1
  17.7 0.1 select_reduce_fusion
  17.8 0.7 fusion.3
  18.5 0.0 copy-done.7
  18.5 0.6 fusion.19
  19.1 35.6 %shard_map.92.patch_rows = bf16[1024,512]{1,0:T(8,128)(2,1)} custom-call(s32[1,3072]{1,0:T(1,128)} %bitcast.14, bf16[4,768,128]{2,1,0:T(8,128)(2,1)} %shard_map.91.slabs), custom_call_target="tpu_custom_call" | custom-call | flops 2415919104 | bytes 7864320 | tf_op jit(solution)/shard_map/pallas_call | solution.py:209
  54.7 0.0 collective-permute-done.refs_1_
  54.7 0.0 copy-done.5
  54.7 0.4 collective-permute-start.1
  55.1 0.1 collective-permute-start.2
  55.3 0.0 all-gather.2.cloned.1.call-done.weights
  55.3 27.8 %shard_map.93.attended = bf16[512,512]{1,0:T(8,128)(2,1)} custom-call(s32[1]{0:T(128)} %bitcast.3.query_from, bf16[1024,512]{1,0:T(8,128)(2,1)} %shard_map.92.patch_rows, f32[1,512]{1,0:T(1,128)} %get-tuple-element.14.gain, bf16[2048,384]{1,0:T(8,128)(2,1)} %all-gather.2.cloned.1.call-done.weights), custom_call_target="tpu_custom_call" | custom-call | flops 17179869184 | bytes 2097152 | tf_op jit(solution)/shard_map/pallas_call | solution.py:565
  83.1 0.0 collective-permute-done.1.refs_2_
  83.1 0.0 copy-start.8
  83.1 0.0 collective-permute-done.2.refs_3_
  83.1 1.0 copy-done.8
  84.1 7.0 %shard_map.94.result = bf16[4,512,128]{2,1,0:T(8,128)(2,1)} custom-call(s32[5]{0:T(128)} %concatenate.10.scalars, bf16[1024,512]{1,0:T(8,128)(2,1)} %shard_map.92.patch_rows, bf16[512,512]{1,0:T(8,128)(2,1)} %shard_map.93.attended, f32[1,512]{1,0:T(1,128)} %get-tuple-element.13.gain, bf16[1152,512]{1,0:T(8,128)(2,1)} %copy-done.5, ...), custom_call_target="tpu_custom_call" | custom-call | flops 2147483648 | bytes 8388608 | tf_op jit(solution)/shard_map/pallas_call | solution.py:634
  91.1 31.9 %shard_map.95.slabs = bf16[4,768,128]{2,1,0:T(8,128)(2,1)} custom-call(s32[1,3072]{1,0:T(1,128)} %bitcast.15, bf16[4,512,128]{2,1,0:T(8,128)(2,1)} %shard_map.94.result), custom_call_target="tpu_custom_call" | custom-call | flops 2415919104 | bytes 7864320 | tf_op jit(solution)/shard_map/pallas_call | solution.py:366
  123.0 3.1 %shard_map.96 = bf16[3072,128]{1,0:T(8,128)(2,1)} custom-call(s32[2,4]{1,0:T(2,128)} %pad_add_fusion.starts, bf16[4,768,128]{2,1,0:T(8,128)(2,1)} %shard_map.95.slabs), custom_call_target="tpu_custom_call" | custom-call | tf_op jit(solution)/shard_map/pallas_call | solution.py:449
  (10 shorter events, 0.2 us)
Async XLA Ops:
  6.5 1.0 copy-start
  6.5 2.2 %copy-start.3 = (bf16[128,512]{1,0:T(8,128)(2,1)S(1)}, bf16[128,512]{1,0:T(8,128)(2,1)}, u32[]{:S(2)}) copy-start(bf16[128,512]{1,0:T(8,128)(2,1)} %param.14) | copy-start | bytes 393220
  6.5 2.2 %copy-start.1 = (bf16[512,512]{1,0:T(8,128)(2,1)S(1)}, bf16[512,512]{1,0:T(8,128)(2,1)}, u32[]{:S(2)}) copy-start(bf16[512,512]{1,0:T(8,128)(2,1)} %param.15) | copy-start | bytes 1572868
  6.5 48.7 %all-gather.2.cloned.1.call-start = ((), (), s32[]{:S(2)}) async-start(), calls=%async_computation | async-start | bytes 1966080 | tf_op jit(solution)/shard_map/all_gather | solution.py:681
  7.5 1.3 copy-start.2
  8.7 3.8 %copy-start.6 = (s32[3072]{0:T(1024)S(1)}, s32[3072]{0:T(1024)}, u32[]{:S(2)}) copy-start(s32[3072]{0:T(1024)} %param.10) | copy-start | bytes 36868
  8.9 45.8 %copy-start.5 = (bf16[1152,512]{1,0:T(8,128)(2,1)}, bf16[1152,512]{1,0:T(8,128)(2,1)S(1)}, u32[]{:S(2)}) copy-start(bf16[1152,512]{1,0:T(8,128)(2,1)S(1)} %constant_dynamic-update-slice_fusion.refs_0_) | copy-start | bytes 3538948
  8.9 45.8 %collective-permute-start = (bf16[1152,512]{1,0:T(8,128)(2,1)S(1)}, bf16[1152,512]{1,0:T(8,128)(2,1)}, u32[]{:S(2)}, u32[]{:S(2)}) collective-permute-start(bf16[1152,512]{1,0:T(8,128)(2,1)S(1)} %constant_dynamic-update-slice_fusion.refs_0_), channel_id=1, source_target_pairs={{0,2},{1,3},{2,0},{3,1},{4,6},{5,7},{6,4},{7,5},{8,10},{9,11},{10,... | collective-permute-start | bytes 3538952 | tf_op jit(solution)/shard_map/ppermute | solution.py:29
  13.4 4.1 %copy-start.4 = (s32[2048]{0:T(1024)S(1)}, s32[2048]{0:T(1024)}, u32[]{:S(2)}) copy-start(s32[2048]{0:T(1024)} %param.11) | copy-start | bytes 24580
  13.4 5.1 %copy-start.7 = (f32[2,512]{1,0:T(2,128)S(1)}, f32[2,512]{1,0:T(2,128)}, u32[]{:S(2)}) copy-start(f32[2,512]{1,0:T(2,128)} %param.17) | copy-start | bytes 12292
  54.7 28.4 %collective-permute-start.1 = (bf16[1152,512]{1,0:T(8,128)(2,1)S(1)}, bf16[1152,512]{1,0:T(8,128)(2,1)S(1)}, u32[]{:S(2)}, u32[]{:S(2)}) collective-permute-start(bf16[1152,512]{1,0:T(8,128)(2,1)S(1)} %constant_dynamic-update-slice_fusion.refs_0_), channel_id=1, source_target_pairs={{0,1},{1,0},{2,3},{3,2},{4,5},{5,4},{6,7},{7,6},{8,9},{9,8},{10,11... | collective-permute-start | bytes 3538952 | tf_op jit(solution)/shard_map/ppermute | solution.py:29
  55.1 28.0 %collective-permute-start.2 = (bf16[1152,512]{1,0:T(8,128)(2,1)}, bf16[1152,512]{1,0:T(8,128)(2,1)}, u32[]{:S(2)}, u32[]{:S(2)}) collective-permute-start(bf16[1152,512]{1,0:T(8,128)(2,1)} %collective-permute-done.refs_1_), channel_id=1, source_target_pairs={{0,1},{1,0},{2,3},{3,2},{4,5},{5,4},{6,7},{7,6},{8,9},{9,8},{10,11... | collective-permute-start | bytes 3538952 | tf_op jit(solution)/shard_map/ppermute | solution.py:29
  83.1 1.0 copy-start.8
Sparse Core Ops, SparseCore 0:
  8.9 30.9 all-gather.1

commit v5 on v4

--- a/solution.py
+++ b/solution.py
@@ -93,16 +93,17 @@
     for start in range(0, rows, tile):
         column_index[start : start + tile, :] = jnp.broadcast_to(
             index[:, start : start + tile], (lane_width, tile)
-        ).T
+        ).T.astype(jnp.int16)
 
     def merge(lane, source, first):
         def one_tile(step, carry):
             at = pl.ds(pl.multiple_of(step * tile, tile), tile)
-            mine = column_index[at, :] - lane * slab_rows
-            spots = lax.broadcasted_iota(jnp.int32, (tile, lane_width), 1)
+            mine = column_index[at, :]
+            spots = lax.broadcasted_iota(jnp.int32, (tile, lane_width), 1) + lane * slab_rows
+            one, zero = jnp.ones((), jnp.bfloat16), jnp.zeros((), jnp.bfloat16)
             chosen = jnp.concatenate(
                 [
-                    jnp.where(mine == spots + start, 1.0, 0.0).astype(jnp.bfloat16)
+                    jnp.where(mine == (spots + start).astype(jnp.int16), one, zero)
                     for start in range(0, slab_rows, lane_width)
                 ],
                 axis=1,
@@ -217,7 +218,7 @@
             pltpu.VMEM((rows, width), jnp.bfloat16),
             pltpu.VMEM((parts, PATCH, width), jnp.bfloat16),
             pltpu.VMEM((PATCH, width), jnp.bfloat16),
-            pltpu.VMEM((rows, 128), jnp.int32),
+            pltpu.VMEM((rows, 128), jnp.int16),
             pltpu.SemaphoreType.DMA((lanes,)),
             pltpu.SemaphoreType.DMA((lanes,)),
             pltpu.SemaphoreType.DMA((parts,)),
@@ -333,12 +334,12 @@
 
     def spread(lane, start, stop):
         spots = lax.broadcasted_iota(jnp.int32, (slab_rows, stop - start), 0)
-        chosen = jnp.where(
-            index[:, start:stop] == spots + lane * slab_rows, 1.0, 0.0
-        ).astype(jnp.bfloat16)
+        mine = (index[:, start:stop] - lane * slab_rows).astype(jnp.int16)
+        one, zero = jnp.ones((), jnp.bfloat16), jnp.zeros((), jnp.bfloat16)
+        chosen = jnp.where(mine == spots.astype(jnp.int16), one, zero)
         return jnp.dot(chosen, rows_in[start:stop, :], preferred_element_type=jnp.float32)
 
-    for lane in range(lanes):
+    for lane in (3, 0, 2):
         total[lane] = spread(lane, PATCH, rows)
     for source in range(parts):
         if row_start(source) >= last:
@@ -346,7 +347,7 @@
     for lane in (3, 0, 2):
         leaving[lane] = (total[lane] + spread(lane, 0, PATCH)).astype(jnp.bfloat16)
         lane_copy(lane).start()
-    arrived[1] = (total[1] + spread(1, 0, PATCH)).astype(jnp.bfloat16)
+    arrived[1] = spread(1, 0, rows).astype(jnp.bfloat16)
     for lane in (2, 0, 3):
         lane_copy(lane).wait()
 
@@ -513,7 +514,7 @@
         values[group, :, :lanes] = both[:, lanes:]
         values[group, :, lanes:] = jnp.ones_like(both[:, lanes:])
 
-    heads_once = 4
+    heads_once = group_heads
     chunks = query_rows // query_tile
 
     def some_heads(turn, carry):
@@ -611,9 +612,13 @@
         mixed = term if mixed is None else mixed + term
     hidden = (own + mixed).astype(jnp.bfloat16).astype(jnp.float32)
     normed = layer_norm(hidden, gain[...])
-    total = None
+
+    def widen(group):
+        return jnp.dot(normed, up_weight[group], preferred_element_type=jnp.float32)
+
+    total, expanded = None, widen(0)
     for group in range(groups):
-        expanded = jnp.dot(normed, up_weight[group], preferred_element_type=jnp.float32)
+        later = widen(group + 1) if group + 1 < groups else None
         expanded = (
             0.5 * expanded * (1.0 + lax.erf(expanded * math.sqrt(0.5)))
         ).astype(jnp.bfloat16)
@@ -621,6 +626,7 @@
             expanded, down_weight[group], preferred_element_type=jnp.float32
         ).astype(jnp.bfloat16).astype(jnp.float32)
         total = term if total is None else total + term
+        expanded = later
     final = (hidden + total).astype(jnp.bfloat16)
     width = result.shape[2]
     for part in range(result.shape[0]):

time: 134 us -> 133 us (level)
  Pallas kernels: 109 us -> 107 us
    pallas_call x1, Pallas kernels: 27.8 us -> 26.3 us  [attention(): pl.pallas_call(functools.partial(attention_kernel, head_dim, query_rows /...]
where the time goes in v5:
time: 133 us; the launch traced here: 131 us
  Pallas kernels  107 us (80%)
  between operations  14.2 us (11%)
  starting transfers between devices  3.58 us (3%)
  local copies, waits for them, and re-layouts  3.29 us (2%)
  other arithmetic  1.78 us (1%)
    pallas_call x1, Pallas kernels, enter(): pl.pallas_call(functools.partial(enter_kernel, bricks, parts), out_shape=...  35.6 us
    pallas_call x1, Pallas kernels, leave(): pl.pallas_call(functools.partial(leave_kernel, bricks, parts), out_shape=...  31.8 us
    pallas_call x1, Pallas kernels, attention(): pl.pallas_call(functools.partial(attention_kernel, head_dim, query_rows /...  26.3 us
    pallas_call x1, Pallas kernels, mlp(): pl.pallas_call(mlp_kernel, out_shape=jax.ShapeDtypeStruct((groups, rows,...  6.92 us
    ppermute x3, starting transfers between devices, passed(): return lax.ppermute(value, 'mp', pairs)  3.58 us
    pallas_call x1, Pallas kernels, cut(): pl.pallas_call(cut_kernel, out_shape=jax.ShapeDtypeStruct((lanes, slab_ro...  3.5 us
    pallas_call x1, Pallas kernels, place(): pl.pallas_call(place_kernel, out_shape=jax.ShapeDtypeStruct((capacity, wi...  3.1 us
  transfers between devices with their start and end apart: 4, of which 0 were waited for; matrix products, arithmetic and copies ran while one was open for 2% of the time, Pallas kernels for 50%

profile of v5, /device:TPU:0, one launch (start us, length us, event | category | flops | bytes accessed | tf_op | source)
XLA Modules:
  0.0 131.3 jit_solution(2835559940080197154)
XLA Ops:
  6.5 0.0 copy-start
  6.5 0.0 copy-start.3
  6.5 0.0 copy-start.1
  6.5 0.0 all-gather.2.cloned.1.call-start
  6.6 1.0 copy-done
  7.5 0.0 copy-start.2
  7.5 1.2 fusion
  8.7 0.0 all-gather.2.cloned.1.call-update
  8.7 0.0 copy-done.3
  8.7 0.0 copy-start.6
  8.8 0.0 copy-done.1
  8.8 0.0 copy-done.2
  8.9 0.0 copy-start.5
  8.9 3.0 %collective-permute-start = (bf16[1152,512]{1,0:T(8,128)(2,1)S(1)}, bf16[1152,512]{1,0:T(8,128)(2,1)}, u32[]{:S(2)}, u32[]{:S(2)}) collective-permute-start(bf16[1152,512]{1,0:T(8,128)(2,1)S(1)} %constant_dynamic-update-slice_fusion.refs_0_), channel_id=1, source_target_pairs={{0,2},{1,3},{2,0},{3,1},{4,6},{5,7},{6,4},{7,5},{8,10},{9,11},{10,... | collective-permute-start | bytes 3538952 | tf_op jit(solution)/shard_map/ppermute | solution.py:29
  12.6 0.0 copy-done.6
  12.6 0.2 convert_reduce_fusion
  12.8 0.6 pad_add_fusion.starts
  13.4 0.0 copy-start.4
  13.4 0.0 copy-start.7
  13.4 3.5 %shard_map.91.slabs = bf16[4,768,128]{2,1,0:T(8,128)(2,1)} custom-call(s32[2,4]{1,0:T(2,128)} %pad_add_fusion.starts, bf16[3072,512]{1,0:T(8,128)(2,1)} %voxel_feats.1), custom_call_target="tpu_custom_call" | custom-call | tf_op jit(solution)/shard_map/pallas_call | solution.py:421
  16.9 0.6 concatenate.10.scalars
  17.5 0.0 copy-done.4
  17.5 0.1 select_reduce_fusion.1
  17.7 0.1 select_reduce_fusion
  17.8 0.7 fusion.3
  18.5 0.0 copy-done.7
  18.5 0.6 fusion.19
  19.1 35.6 %shard_map.92.patch_rows = bf16[1024,512]{1,0:T(8,128)(2,1)} custom-call(s32[1,3072]{1,0:T(1,128)} %bitcast.14, bf16[4,768,128]{2,1,0:T(8,128)(2,1)} %shard_map.91.slabs), custom_call_target="tpu_custom_call" | custom-call | flops 2415919104 | bytes 7864320 | tf_op jit(solution)/shard_map/pallas_call | solution.py:210
  54.7 0.0 collective-permute-done.refs_1_
  54.7 0.0 copy-done.5
  54.7 0.4 collective-permute-start.1
  55.1 0.1 collective-permute-start.2
  55.3 0.0 all-gather.2.cloned.1.call-done.weights
  55.3 26.3 %shard_map.93.attended = bf16[512,512]{1,0:T(8,128)(2,1)} custom-call(s32[1]{0:T(128)} %bitcast.3.query_from, bf16[1024,512]{1,0:T(8,128)(2,1)} %shard_map.92.patch_rows, f32[1,512]{1,0:T(1,128)} %get-tuple-element.14.gain, bf16[2048,384]{1,0:T(8,128)(2,1)} %all-gather.2.cloned.1.call-done.weights), custom_call_target="tpu_custom_call" | custom-call | flops 17179869184 | bytes 2097152 | tf_op jit(solution)/shard_map/pallas_call | solution.py:566
  81.6 0.0 collective-permute-done.1.refs_2_
  81.6 0.0 copy-start.8
  81.6 0.0 collective-permute-done.2.refs_3_
  81.6 1.0 copy-done.8
  82.6 6.9 %shard_map.94.result = bf16[4,512,128]{2,1,0:T(8,128)(2,1)} custom-call(s32[5]{0:T(128)} %concatenate.10.scalars, bf16[1024,512]{1,0:T(8,128)(2,1)} %shard_map.92.patch_rows, bf16[512,512]{1,0:T(8,128)(2,1)} %shard_map.93.attended, f32[1,512]{1,0:T(1,128)} %get-tuple-element.13.gain, bf16[1152,512]{1,0:T(8,128)(2,1)} %copy-done.5, ...), custom_call_target="tpu_custom_call" | custom-call | flops 2147483648 | bytes 8388608 | tf_op jit(solution)/shard_map/pallas_call | solution.py:640
  89.5 31.8 %shard_map.95.slabs = bf16[4,768,128]{2,1,0:T(8,128)(2,1)} custom-call(s32[1,3072]{1,0:T(1,128)} %bitcast.15, bf16[4,512,128]{2,1,0:T(8,128)(2,1)} %shard_map.94.result), custom_call_target="tpu_custom_call" | custom-call | flops 2415919104 | bytes 7864320 | tf_op jit(solution)/shard_map/pallas_call | solution.py:367
  121.3 3.1 %shard_map.96 = bf16[3072,128]{1,0:T(8,128)(2,1)} custom-call(s32[2,4]{1,0:T(2,128)} %pad_add_fusion.starts, bf16[4,768,128]{2,1,0:T(8,128)(2,1)} %shard_map.95.slabs), custom_call_target="tpu_custom_call" | custom-call | tf_op jit(solution)/shard_map/pallas_call | solution.py:450
  (10 shorter events, 0.2 us)
Async XLA Ops:
  6.5 1.0 copy-start
  6.5 2.2 %copy-start.3 = (bf16[128,512]{1,0:T(8,128)(2,1)S(1)}, bf16[128,512]{1,0:T(8,128)(2,1)}, u32[]{:S(2)}) copy-start(bf16[128,512]{1,0:T(8,128)(2,1)} %param.14) | copy-start | bytes 393220
  6.5 2.2 %copy-start.1 = (bf16[512,512]{1,0:T(8,128)(2,1)S(1)}, bf16[512,512]{1,0:T(8,128)(2,1)}, u32[]{:S(2)}) copy-start(bf16[512,512]{1,0:T(8,128)(2,1)} %param.15) | copy-start | bytes 1572868
  6.5 48.7 %all-gather.2.cloned.1.call-start = ((), (), s32[]{:S(2)}) async-start(), calls=%async_computation | async-start | bytes 1966080 | tf_op jit(solution)/shard_map/all_gather | solution.py:687
  7.5 1.3 copy-start.2
  8.7 3.8 %copy-start.6 = (s32[3072]{0:T(1024)S(1)}, s32[3072]{0:T(1024)}, u32[]{:S(2)}) copy-start(s32[3072]{0:T(1024)} %param.10) | copy-start | bytes 36868
  8.9 45.8 %copy-start.5 = (bf16[1152,512]{1,0:T(8,128)(2,1)}, bf16[1152,512]{1,0:T(8,128)(2,1)S(1)}, u32[]{:S(2)}) copy-start(bf16[1152,512]{1,0:T(8,128)(2,1)S(1)} %constant_dynamic-update-slice_fusion.refs_0_) | copy-start | bytes 3538948
  8.9 45.8 %collective-permute-start = (bf16[1152,512]{1,0:T(8,128)(2,1)S(1)}, bf16[1152,512]{1,0:T(8,128)(2,1)}, u32[]{:S(2)}, u32[]{:S(2)}) collective-permute-start(bf16[1152,512]{1,0:T(8,128)(2,1)S(1)} %constant_dynamic-update-slice_fusion.refs_0_), channel_id=1, source_target_pairs={{0,2},{1,3},{2,0},{3,1},{4,6},{5,7},{6,4},{7,5},{8,10},{9,11},{10,... | collective-permute-start | bytes 3538952 | tf_op jit(solution)/shard_map/ppermute | solution.py:29
  13.4 4.1 %copy-start.4 = (s32[2048]{0:T(1024)S(1)}, s32[2048]{0:T(1024)}, u32[]{:S(2)}) copy-start(s32[2048]{0:T(1024)} %param.11) | copy-start | bytes 24580
  13.4 5.1 %copy-start.7 = (f32[2,512]{1,0:T(2,128)S(1)}, f32[2,512]{1,0:T(2,128)}, u32[]{:S(2)}) copy-start(f32[2,512]{1,0:T(2,128)} %param.17) | copy-start | bytes 12292
  54.7 26.9 %collective-permute-start.1 = (bf16[1152,512]{1,0:T(8,128)(2,1)S(1)}, bf16[1152,512]{1,0:T(8,128)(2,1)S(1)}, u32[]{:S(2)}, u32[]{:S(2)}) collective-permute-start(bf16[1152,512]{1,0:T(8,128)(2,1)S(1)} %constant_dynamic-update-slice_fusion.refs_0_), channel_id=1, source_target_pairs={{0,1},{1,0},{2,3},{3,2},{4,5},{5,4},{6,7},{7,6},{8,9},{9,8},{10,11... | collective-permute-start | bytes 3538952 | tf_op jit(solution)/shard_map/ppermute | solution.py:29
  55.1 26.5 %collective-permute-start.2 = (bf16[1152,512]{1,0:T(8,128)(2,1)}, bf16[1152,512]{1,0:T(8,128)(2,1)}, u32[]{:S(2)}, u32[]{:S(2)}) collective-permute-start(bf16[1152,512]{1,0:T(8,128)(2,1)} %collective-permute-done.refs_1_), channel_id=1, source_target_pairs={{0,1},{1,0},{2,3},{3,2},{4,5},{5,4},{6,7},{7,6},{8,9},{9,8},{10,11... | collective-permute-start | bytes 3538952 | tf_op jit(solution)/shard_map/ppermute | solution.py:29
  81.6 1.0 copy-start.8
Sparse Core Ops, SparseCore 0:
  8.9 30.9 all-gather.1

commit v6 on v5

--- a/solution.py
+++ b/solution.py
@@ -34,12 +34,11 @@
     return jnp.where(value >= count, value - count, value)
 
 
-def greet_all(bricks, parts, wide):
+def greet_all(bricks, parts):
     brick, part = lax.axis_index("brick"), lax.axis_index("mp")
     barrier = pltpu.get_barrier_semaphore()
     peers = [(0, step) for step in range(1, parts)]
-    peers += [(away, step) for away in (-1, 1) for step in range(parts if wide else 1)]
-    peers += [(-2, 0), (2, 0)]
+    peers += [(away, 0) for away in (-2, -1, 1, 2)]
     for away, step in peers:
         pl.semaphore_signal(
             barrier,
@@ -76,7 +75,7 @@
     rows = index.shape[1]
     tile = 1024
     lane_width = column_index.shape[1]
-    greet_all(bricks, parts, False)
+    greet_all(bricks, parts)
 
     def lane_copy(lane):
         return pltpu.make_async_remote_copy(
@@ -260,22 +259,19 @@
     quarter = result.shape[1]
     rows = rows_in.shape[0]
     last = rows - PATCH
-    greet_all(bricks, parts, True)
+    greet_all(bricks, parts)
 
     def row_start(source):
         return PATCH + source * quarter
 
-    def tail_copy(step):
-        target = lax.rem(part + step, parts)
-        start = pl.multiple_of(jnp.maximum(row_start(part) - last, 0), quarter)
-        return pltpu.make_async_remote_copy(
-            src_ref=result.at[target],
-            dst_ref=rows_in.at[pl.ds(start, quarter)],
-            send_sem=tail_send.at[step],
-            recv_sem=tail_recv.at[part],
-            device_id=(lax.rem(brick + 1, bricks), target),
-            device_id_type=MESH,
-        )
+    tail_copy = pltpu.make_async_remote_copy(
+        src_ref=rows_in.at[pl.ds(last, PATCH)],
+        dst_ref=rows_in.at[pl.ds(0, PATCH)],
+        send_sem=tail_send.at[0],
+        recv_sem=tail_recv.at[0],
+        device_id=(lax.rem(brick + 1, bricks), part),
+        device_id_type=MESH,
+    )
 
     def window_copy(step):
         target = lax.rem(part + step, parts)
@@ -289,16 +285,6 @@
             device_id_type=MESH,
         )
 
-    def tail_arrival(source):
-        return pltpu.make_async_remote_copy(
-            src_ref=result.at[0],
-            dst_ref=rows_in.at[pl.ds(row_start(source) - last, quarter)],
-            send_sem=tail_send.at[0],
-            recv_sem=tail_recv.at[source],
-            device_id=(lax.rem(brick + 1, bricks), part),
-            device_id_type=MESH,
-        )
-
     def window_arrival(step):
         source = lax.rem(part - step + parts, parts)
         return pltpu.make_async_remote_copy(
@@ -310,18 +296,12 @@
             device_id_type=MESH,
         )
 
-    sends_tail = row_start(part) >= last
-
-    @pl.when(sends_tail)
-    def _():
-        for step in range(parts):
-            tail_copy(step).start()
-
     for step in range(1, parts):
         window_copy(step).start()
     rows_in[pl.ds(pl.multiple_of(row_start(part), quarter), quarter), :] = result[part]
     for step in range(1, parts):
         window_arrival(step).wait_recv()
+    tail_copy.start()
     def lane_copy(lane):
         return pltpu.make_async_remote_copy(
             src_ref=leaving.at[lane],
@@ -341,9 +321,7 @@
 
     for lane in (3, 0, 2):
         total[lane] = spread(lane, PATCH, rows)
-    for source in range(parts):
-        if row_start(source) >= last:
-            tail_arrival(source).wait_recv()
+    tail_copy.wait_recv()
     for lane in (3, 0, 2):
         leaving[lane] = (total[lane] + spread(lane, 0, PATCH)).astype(jnp.bfloat16)
         lane_copy(lane).start()
@@ -354,10 +332,7 @@
     for step in range(1, parts):
         window_copy(step).wait_send()
 
-    @pl.when(sends_tail)
-    def _():
-        for step in range(parts):
-            tail_copy(step).wait_send()
+    tail_copy.wait_send()
 
 
 def leave(index, result, bricks, lanes, slab_rows):

time: 133 us -> 131 us (0.985)
  no operation moved by 1% of the time
where the time goes in v6:
time: 131 us
  Pallas kernels  106 us (81%)
  between operations  14.2 us (11%)
  starting transfers between devices  3.58 us (3%)
  local copies, waits for them, and re-layouts  3.29 us (3%)
  other arithmetic  1.78 us (1%)
    pallas_call x1, Pallas kernels, enter(): pl.pallas_call(functools.partial(enter_kernel, bricks, parts), out_shape=...  35.6 us
    pallas_call x1, Pallas kernels, leave(): pl.pallas_call(functools.partial(leave_kernel, bricks, parts), out_shape=...  31.1 us
    pallas_call x1, Pallas kernels, attention(): pl.pallas_call(functools.partial(attention_kernel, head_dim, query_rows /...  26.3 us
    pallas_call x1, Pallas kernels, mlp(): pl.pallas_call(mlp_kernel, out_shape=jax.ShapeDtypeStruct((groups, rows,...  6.92 us
    ppermute x3, starting transfers between devices, passed(): return lax.ppermute(value, 'mp', pairs)  3.58 us
    pallas_call x1, Pallas kernels, cut(): pl.pallas_call(cut_kernel, out_shape=jax.ShapeDtypeStruct((lanes, slab_ro...  3.5 us
    pallas_call x1, Pallas kernels, place(): pl.pallas_call(place_kernel, out_shape=jax.ShapeDtypeStruct((capacity, wi...  3.1 us
  transfers between devices with their start and end apart: 4, of which 0 were waited for; matrix products, arithmetic and copies ran while one was open for 2% of the time, Pallas kernels for 50%

profile of v6, /device:TPU:0, one launch (start us, length us, event | category | flops | bytes accessed | tf_op | source)
XLA Modules:
  0.0 130.5 jit_solution(10563844913781932872)
XLA Ops:
  6.5 0.0 copy-start
  6.5 0.0 copy-start.3
  6.5 0.0 copy-start.1
  6.5 0.0 all-gather.2.cloned.1.call-start
  6.6 1.0 copy-done
  7.5 0.0 copy-start.2
  7.5 1.2 fusion
  8.7 0.0 all-gather.2.cloned.1.call-update
  8.7 0.0 copy-done.3
  8.7 0.0 copy-start.6
  8.8 0.0 copy-done.1
  8.8 0.0 copy-done.2
  8.9 0.0 copy-start.5
  8.9 3.0 %collective-permute-start = (bf16[1152,512]{1,0:T(8,128)(2,1)S(1)}, bf16[1152,512]{1,0:T(8,128)(2,1)}, u32[]{:S(2)}, u32[]{:S(2)}) collective-permute-start(bf16[1152,512]{1,0:T(8,128)(2,1)S(1)} %constant_dynamic-update-slice_fusion.refs_0_), channel_id=1, source_target_pairs={{0,2},{1,3},{2,0},{3,1},{4,6},{5,7},{6,4},{7,5},{8,10},{9,11},{10,... | collective-permute-start | bytes 3538952 | tf_op jit(solution)/shard_map/ppermute | solution.py:29
  12.6 0.0 copy-done.6
  12.6 0.2 convert_reduce_fusion
  12.8 0.6 pad_add_fusion.starts
  13.4 0.0 copy-start.4
  13.4 0.0 copy-start.7
  13.4 3.5 %shard_map.91.slabs = bf16[4,768,128]{2,1,0:T(8,128)(2,1)} custom-call(s32[2,4]{1,0:T(2,128)} %pad_add_fusion.starts, bf16[3072,512]{1,0:T(8,128)(2,1)} %voxel_feats.1), custom_call_target="tpu_custom_call" | custom-call | tf_op jit(solution)/shard_map/pallas_call | solution.py:396
  16.9 0.6 concatenate.10.scalars
  17.5 0.0 copy-done.4
  17.5 0.1 select_reduce_fusion.1
  17.7 0.1 select_reduce_fusion
  17.8 0.7 fusion.3
  18.5 0.0 copy-done.7
  18.5 0.6 fusion.19
  19.1 35.6 %shard_map.92.patch_rows = bf16[1024,512]{1,0:T(8,128)(2,1)} custom-call(s32[1,3072]{1,0:T(1,128)} %bitcast.14, bf16[4,768,128]{2,1,0:T(8,128)(2,1)} %shard_map.91.slabs), custom_call_target="tpu_custom_call" | custom-call | flops 2415919104 | bytes 7864320 | tf_op jit(solution)/shard_map/pallas_call | solution.py:209
  54.7 0.0 collective-permute-done.refs_1_
  54.7 0.0 copy-done.5
  54.7 0.4 collective-permute-start.1
  55.1 0.1 collective-permute-start.2
  55.3 0.0 all-gather.2.cloned.1.call-done.weights
  55.3 26.3 %shard_map.93.attended = bf16[512,512]{1,0:T(8,128)(2,1)} custom-call(s32[1]{0:T(128)} %bitcast.3.query_from, bf16[1024,512]{1,0:T(8,128)(2,1)} %shard_map.92.patch_rows, f32[1,512]{1,0:T(1,128)} %get-tuple-element.14.gain, bf16[2048,384]{1,0:T(8,128)(2,1)} %all-gather.2.cloned.1.call-done.weights), custom_call_target="tpu_custom_call" | custom-call | flops 17179869184 | bytes 2097152 | tf_op jit(solution)/shard_map/pallas_call | solution.py:541
  81.6 0.0 collective-permute-done.1.refs_2_
  81.6 0.0 copy-start.8
  81.6 0.0 collective-permute-done.2.refs_3_
  81.6 1.0 copy-done.8
  82.6 6.9 %shard_map.94.result = bf16[4,512,128]{2,1,0:T(8,128)(2,1)} custom-call(s32[5]{0:T(128)} %concatenate.10.scalars, bf16[1024,512]{1,0:T(8,128)(2,1)} %shard_map.92.patch_rows, bf16[512,512]{1,0:T(8,128)(2,1)} %shard_map.93.attended, f32[1,512]{1,0:T(1,128)} %get-tuple-element.13.gain, bf16[1152,512]{1,0:T(8,128)(2,1)} %copy-done.5, ...), custom_call_target="tpu_custom_call" | custom-call | flops 2147483648 | bytes 8388608 | tf_op jit(solution)/shard_map/pallas_call | solution.py:615
  89.5 31.1 %shard_map.95.slabs = bf16[4,768,128]{2,1,0:T(8,128)(2,1)} custom-call(s32[1,3072]{1,0:T(1,128)} %bitcast.15, bf16[4,512,128]{2,1,0:T(8,128)(2,1)} %shard_map.94.result), custom_call_target="tpu_custom_call" | custom-call | flops 2415919104 | bytes 7864320 | tf_op jit(solution)/shard_map/pallas_call | solution.py:342
  120.6 3.1 %shard_map.96 = bf16[3072,128]{1,0:T(8,128)(2,1)} custom-call(s32[2,4]{1,0:T(2,128)} %pad_add_fusion.starts, bf16[4,768,128]{2,1,0:T(8,128)(2,1)} %shard_map.95.slabs), custom_call_target="tpu_custom_call" | custom-call | tf_op jit(solution)/shard_map/pallas_call | solution.py:425
  (10 shorter events, 0.2 us)
Async XLA Ops:
  6.5 1.0 copy-start
  6.5 2.2 %copy-start.3 = (bf16[128,512]{1,0:T(8,128)(2,1)S(1)}, bf16[128,512]{1,0:T(8,128)(2,1)}, u32[]{:S(2)}) copy-start(bf16[128,512]{1,0:T(8,128)(2,1)} %param.14) | copy-start | bytes 393220
  6.5 2.2 %copy-start.1 = (bf16[512,512]{1,0:T(8,128)(2,1)S(1)}, bf16[512,512]{1,0:T(8,128)(2,1)}, u32[]{:S(2)}) copy-start(bf16[512,512]{1,0:T(8,128)(2,1)} %param.15) | copy-start | bytes 1572868
  6.5 48.7 %all-gather.2.cloned.1.call-start = ((), (), s32[]{:S(2)}) async-start(), calls=%async_computation | async-start | bytes 1966080 | tf_op jit(solution)/shard_map/all_gather | solution.py:662
  7.5 1.3 copy-start.2
  8.7 3.8 %copy-start.6 = (s32[3072]{0:T(1024)S(1)}, s32[3072]{0:T(1024)}, u32[]{:S(2)}) copy-start(s32[3072]{0:T(1024)} %param.10) | copy-start | bytes 36868
  8.9 45.8 %copy-start.5 = (bf16[1152,512]{1,0:T(8,128)(2,1)}, bf16[1152,512]{1,0:T(8,128)(2,1)S(1)}, u32[]{:S(2)}) copy-start(bf16[1152,512]{1,0:T(8,128)(2,1)S(1)} %constant_dynamic-update-slice_fusion.refs_0_) | copy-start | bytes 3538948
  8.9 45.8 %collective-permute-start = (bf16[1152,512]{1,0:T(8,128)(2,1)S(1)}, bf16[1152,512]{1,0:T(8,128)(2,1)}, u32[]{:S(2)}, u32[]{:S(2)}) collective-permute-start(bf16[1152,512]{1,0:T(8,128)(2,1)S(1)} %constant_dynamic-update-slice_fusion.refs_0_), channel_id=1, source_target_pairs={{0,2},{1,3},{2,0},{3,1},{4,6},{5,7},{6,4},{7,5},{8,10},{9,11},{10,... | collective-permute-start | bytes 3538952 | tf_op jit(solution)/shard_map/ppermute | solution.py:29
  13.4 4.1 %copy-start.4 = (s32[2048]{0:T(1024)S(1)}, s32[2048]{0:T(1024)}, u32[]{:S(2)}) copy-start(s32[2048]{0:T(1024)} %param.11) | copy-start | bytes 24580
  13.4 5.1 %copy-start.7 = (f32[2,512]{1,0:T(2,128)S(1)}, f32[2,512]{1,0:T(2,128)}, u32[]{:S(2)}) copy-start(f32[2,512]{1,0:T(2,128)} %param.17) | copy-start | bytes 12292
  54.7 26.9 %collective-permute-start.1 = (bf16[1152,512]{1,0:T(8,128)(2,1)S(1)}, bf16[1152,512]{1,0:T(8,128)(2,1)S(1)}, u32[]{:S(2)}, u32[]{:S(2)}) collective-permute-start(bf16[1152,512]{1,0:T(8,128)(2,1)S(1)} %constant_dynamic-update-slice_fusion.refs_0_), channel_id=1, source_target_pairs={{0,1},{1,0},{2,3},{3,2},{4,5},{5,4},{6,7},{7,6},{8,9},{9,8},{10,11... | collective-permute-start | bytes 3538952 | tf_op jit(solution)/shard_map/ppermute | solution.py:29
  55.1 26.5 %collective-permute-start.2 = (bf16[1152,512]{1,0:T(8,128)(2,1)}, bf16[1152,512]{1,0:T(8,128)(2,1)}, u32[]{:S(2)}, u32[]{:S(2)}) collective-permute-start(bf16[1152,512]{1,0:T(8,128)(2,1)} %collective-permute-done.refs_1_), channel_id=1, source_target_pairs={{0,1},{1,0},{2,3},{3,2},{4,5},{5,4},{6,7},{7,6},{8,9},{9,8},{10,11... | collective-permute-start | bytes 3538952 | tf_op jit(solution)/shard_map/ppermute | solution.py:29
  81.6 1.0 copy-start.8
Sparse Core Ops, SparseCore 0:
  8.9 30.9 all-gather.1
